TPU v7x, 512 devices: a whole 4x8x8 slice. The times are simulated.
512 devices in a mesh: panel: 2 (over x_hi), lat: 16 (over z, core), lon: 16 (over x_lo, y).
Axes of the slice: x: 4 (x_hi: 2, x_lo: 2; x = x_hi * 2 + x_lo), y: 8, z: 8, core: 2. Of those that a mesh axis runs over, the one named last changes fastest.
Arguments:
- state: float32 [2, 8, 4, 256, 768], P('panel', None, None, 'lat', 'lon'), as said below
- donor_cell: int32 [2, 16, 16, 33], P('panel', 'lat', 'lon'), may hold values from 0 to 767, as said below
- donor_weights: float32 [2, 16, 16, 4, 33], P('panel', 'lat', 'lon'), as said below
- donor_turn: float32 [2, 16, 16, 33], P('panel', 'lat', 'lon'), may hold values from -3.140625 to 3.140625
- border_source: int32 [2, 8256], P('panel'), may hold values from 0 to 8446, as said below
- diffusion: float32 [2], replicated, may hold values from 0.01 to 0.1
Outputs:
- accumulated: float32 [2, 8, 4, 256, 768], P('panel', None, None, 'lat', 'lon')
- section_three: float32 [2, 8, 4, 256, 768], P('panel', None, None, 'lat', 'lon')
Inputs may be any that keep to these rules, and one draw needn't show every extreme that they name: `state`: eight fields in order: log density, velocity (r, theta, phi), magnetic field (r, theta, phi), pressure; pressure is positive. `donor_cell`: c names the cell at row c // 48, column c % 48 of the block; the cells one row and one column further lie inside the panel. `donor_weights`: the four weights of a slot are nonnegative and sum to one. `border_source`: entry n of panel p names slot s % 33 of block s // 33 of the other panel, blocks numbered colatitude-major; no slot is named twice; each block serves 33 or 32 ghost cells, from its first slots.
All inputs are finite; a program needn't handle non-finite values.
Results may differ from a plain program's by a relative error of at most 0.00002.
Values sent between devices are 32-bit elements; how exact they have to be, the bound alone decides.
No kernel may reach another device: no remote copies, remote signals or barrier semaphores. Data moves between devices by JAX's collectives and lax.ppermute only.
A program may use at most 64 MiB of HBM per device.

v0:
```python
import math

import jax
import jax.numpy as jnp
from jax import lax
from jax.experimental import pallas as pl
from jax.experimental.pallas import tpu as pltpu
from jax.sharding import PartitionSpec as P

GAMMA = 5.0 / 3.0
RADIAL_STEP = 0.65 / 32.0
FIELDS = 8
LEVELS = 4
PLANES = FIELDS * LEVELS
PAIRS = PLANES // 2
LOW_LEVEL = (0, 1)
HIGH_LEVEL = (3, 2)
ROWS = 16
COLS = 48
SLOTS = 33
LATS = 16
LONS = 16
ROOM = 63
WIDE = 128
HALF = 64
TALL = ROWS + 16
MID = ROWS + 8
BAND = 4 * HALF
SIDE = 4 * TALL
CHUNK = BAND + SIDE
PEERS = 16
PACKED = 32
MESSAGE = 9 * WIDE
TAIL = 8 * WIDE
FLAG = TAIL + HALF - 1
CHOICE_TILES = PEERS * PACKED // WIDE
CHOICE_DEPTH = (CHOICE_TILES + 1) * WIDE
DEPTH = PEERS * HALF
PANEL_ROWS = ROWS * LATS
PANEL_COLS = COLS * LONS
DTHETA = 0.5 * math.pi / PANEL_ROWS
DPHI = 1.5 * math.pi / PANEL_COLS
FINEST = min(DTHETA, DPHI)
TIME_STEP = 0.1 * FINEST
RADII = [0.35 + 0.65 * (k + 16 - LEVELS // 2 + 0.5) / 32.0 for k in range(LEVELS)]
VMEM = pl.BlockSpec(memory_space=pltpu.VMEM)
SMEM = pl.BlockSpec(memory_space=pltpu.SMEM)
MIB = 1024 * 1024


def iota(shape, axis):
    return lax.broadcasted_iota(jnp.int32, shape, axis)


def column_of(shape):
    return iota(shape, len(shape) - 1) & (HALF - 1)


def turn(value, lanes):
    return pltpu.roll(value, lanes % WIDE, 1) if lanes % WIDE else value


def split_dot(left, right):
    total = None
    for _ in range(3):
        part = left.astype(jnp.bfloat16)
        left = left - part.astype(jnp.float32)
        term = jnp.dot(part, right, preferred_element_type=jnp.float32)
        total = term if total is None else total + term
    return total


def donor_message(planes, pick, mix, spin):
    chosen = split_dot(planes, pick).reshape(PAIRS, MID, 2 * WIDE)
    both = jnp.sum(chosen * mix[None], axis=1)
    both = jnp.concatenate([both[:, :WIDE], both[:, WIDE:]], axis=0)
    mixed = both + pltpu.roll(both, HALF, 1)
    cosine = spin[0:1]
    sine = spin[1:2]
    at = (iota((PLANES, WIDE), 0) & (PAIRS - 1)) // 2
    theta = (at == 2) | (at == 5)
    phi = (at == 3) | (at == 6)
    other = jnp.where(theta, pltpu.roll(mixed, PLANES - 2, 0), -pltpu.roll(mixed, 2, 0))
    turned = jnp.where(theta | phi, cosine * mixed + sine * other, mixed)
    return jnp.where(iota((PAIRS, WIDE), 1) < HALF, turned[:PAIRS], turned[PAIRS:])


def post_message(place_ref, packed, flag, out_ref):
    panel = place_ref[0]
    lane = iota((16, WIDE), 1)
    column = lane & (HALF - 1)
    dense = jnp.where(column[:8] < PACKED, packed[:8], turn(packed[8:], PACKED))
    last = jnp.where(
        lane < HALF, packed[:, PACKED : PACKED + 1], packed[:, HALF + PACKED : HALF + PACKED + 1]
    )
    tail = jnp.sum(jnp.where(column == iota((16, WIDE), 0), last, 0.0), axis=0, keepdims=True)
    blank = jnp.where(lane[:1] == FLAG - TAIL, flag, 0.0)
    tail = jnp.where(lane[:1] == FLAG - TAIL, flag, tail)
    zero = jnp.zeros((1, WIDE), jnp.float32)
    for row in range(9):
        full = dense[row : row + 1] if row < 8 else tail
        empty = zero if row < 8 else blank
        at = slice(row * WIDE, (row + 1) * WIDE)
        out_ref[pl.ds((1 - panel) * PEERS, PEERS), :, at] = jnp.broadcast_to(
            full[None], (PEERS, 1, WIDE)
        )
        out_ref[pl.ds(panel * PEERS, PEERS), :, at] = jnp.broadcast_to(
            empty[None], (PEERS, 1, WIDE)
        )


def cut_kernel(state_ref, held_ref, south_ref, east_ref, corner_ref, plane_ref):
    for plane in range(PLANES):
        plane_ref[plane, :, :COLS] = state_ref[plane // LEVELS, plane % LEVELS]
    lane = iota((ROWS, WIDE), 1)
    column = column_of((ROWS, WIDE))
    own = (column >= 8) & (column < 8 + COLS)
    for pair in range(PAIRS):
        field, which = pair // 2, pair % 2
        low = turn(plane_ref[field * LEVELS + LOW_LEVEL[which]], 8)
        high = turn(plane_ref[field * LEVELS + HIGH_LEVEL[which]], HALF + 8)
        tile = jnp.where(own, jnp.where(lane < HALF, low, high), 0.0)
        held_ref[pair] = tile
        south_ref[pair] = tile[:8]
    for group in range(2):
        columns = jnp.zeros((ROWS, WIDE), jnp.float32)
        for which in range(8):
            moved = turn(held_ref[8 * group + which], 8 * which - 8)
            columns = jnp.where(column // 8 == which, moved, columns)
        east_ref[group] = columns
        corner_ref[group] = columns[:8]


def donor_tables(donor_ref, pick_ref, mix_ref, spin_ref, line_ref):
    late = iota((1, WIDE), 1) >= HALF

    def twice(value, fill):
        line_ref[...] = jnp.full((1, WIDE), fill, jnp.float32)
        line_ref[:, :SLOTS] = value
        line = line_ref[...]
        return jnp.where(late, pltpu.roll(line, HALF, 1), line)

    cell = twice(donor_ref[0:1], -10.0 * COLS)
    row_at = jnp.floor((cell + 0.5) * (1.0 / COLS))
    col_at = cell - row_at * COLS + jnp.where(late, 1.0, 0.0)
    upper = jnp.where(late, twice(donor_ref[2:3], 0.0), twice(donor_ref[1:2], 0.0))
    lower = jnp.where(late, twice(donor_ref[4:5], 0.0), twice(donor_ref[3:4], 0.0))
    angle = twice(donor_ref[5:6], 0.0)
    spin_ref[0:1] = jnp.cos(angle)
    spin_ref[1:2] = jnp.sin(angle)
    lane = iota((WIDE, WIDE), 0).astype(jnp.float32)
    real = jnp.where(row_at >= 0, col_at + 8.0, -1000.0)
    pick_ref[:, :WIDE] = jnp.where(lane == real, 1.0, 0.0).astype(jnp.bfloat16)
    pick_ref[:, WIDE:] = jnp.where(lane == real + HALF, 1.0, 0.0).astype(jnp.bfloat16)
    row = iota((MID, WIDE), 0).astype(jnp.float32)
    mix = jnp.where(row == row_at, upper, 0.0) + jnp.where(row == row_at + 1.0, lower, 0.0)
    mix_ref[:, :WIDE] = mix
    mix_ref[:, WIDE:] = mix


def count_kernel(bands_ref, sides_ref, flag_ref):
    width = bands_ref.shape[1]
    column = iota((width, WIDE), 0) - 4
    start = iota((width, WIDE), 1) * COLS - 8
    within = (column >= start) & (column < start + 64) & (start < PANEL_COLS)
    columns = jnp.where(within, 1.0, 0.0).astype(jnp.bfloat16)
    row = iota((PANEL_ROWS, WIDE), 0)
    start = iota((PANEL_ROWS, WIDE), 1) * ROWS - 8
    within = (row >= start) & (row < start + TALL) & (start < PANEL_ROWS)
    rows = jnp.where(within, 1.0, 0.0).astype(jnp.bfloat16)

    def most(slots, windows):
        ones = []
        for which in range(LATS):
            first = which * LONS * SLOTS
            inside = (slots >= first) & (slots < first + LONS * SLOTS)
            ones.append(jnp.where(inside, 1.0, 0.0))
        ones = jnp.concatenate(ones, axis=0).astype(jnp.bfloat16)
        counts = jnp.dot(ones, windows, preferred_element_type=jnp.float32)
        return jnp.max(jnp.sum(counts.reshape(2 * LATS, 4, WIDE), axis=1))

    total = most(bands_ref[...], columns) + most(sides_ref[...], rows)
    flag_ref[...] = jnp.full(flag_ref.shape, total, jnp.float32)


def donor_kernel(
    place_ref, held_ref, south_ref, east_ref, corner_ref, pick_ref, mix_ref, spin_ref,
    lower_ref, out_ref
):
    column = column_of((ROWS, WIDE))
    beyond = column >= 8 + COLS
    for pair in range(PAIRS):
        group, which = pair // 8, pair % 8
        east = turn(east_ref[group], 8 + COLS - 8 * which)
        corner = turn(corner_ref[group], 8 + COLS - 8 * which)
        lower_ref[pair, :ROWS] = jnp.where(beyond, east, held_ref[pair])
        lower_ref[pair, ROWS:] = jnp.where(beyond[:8], corner, south_ref[pair])
    planes = lower_ref[...].reshape(PAIRS * MID, WIDE)
    packed = donor_message(planes, pick_ref[...], mix_ref[...], spin_ref[...])
    post_message(place_ref, packed, jnp.zeros((1, WIDE), jnp.float32), out_ref)


def last_kernel(lower_ref, west_ref):
    column = column_of((MID, WIDE))
    for group in range(2):
        columns = jnp.zeros((MID, WIDE), jnp.float32)
        for which in range(8):
            moved = turn(lower_ref[8 * group + which], 8 * which - COLS)
            columns = jnp.where(column // 8 == which, moved, columns)
        west_ref[group] = columns


def split_parts(held):
    parts = []
    for _ in range(3):
        part = held.astype(jnp.bfloat16)
        held = held - part.astype(jnp.float32)
        parts.append(part)
    return jnp.concatenate(parts, axis=0)


def join_parts(terms):
    return terms[:PLANES] + terms[PLANES : 2 * PLANES] + terms[2 * PLANES :]


def from_row(place_ref, got_ref):
    base = (1 - place_ref[0]) * PEERS
    part = iota((8, WIDE), 1) // PACKED
    tiles = []
    tails = []
    for tile in range(CHOICE_TILES):
        rows = [jnp.zeros((8, WIDE), jnp.float32)] * 4
        for which in range(4):
            at = base + 4 * tile + which
            message = jnp.concatenate(
                [got_ref[at, :, row * WIDE : (row + 1) * WIDE] for row in range(8)], axis=0
            )
            tails.append(got_ref[at, :, TAIL:])
            for group in range(4):
                moved = turn(message, PACKED * (which - group))
                rows[group] = jnp.where(part == which, moved, rows[group])
        tiles.append(jnp.concatenate(rows, axis=0))
    tails.append(jnp.zeros((WIDE - PEERS, WIDE), jnp.float32))
    tails = jnp.concatenate(tails, axis=0).T
    tiles.append(jnp.concatenate([tails[:PAIRS], tails[HALF : HALF + PAIRS]], axis=0))
    return split_parts(jnp.concatenate(tiles, axis=1))


def rank_of(chosen):
    order = iota((CHUNK, CHUNK), 0) < iota((CHUNK, CHUNK), 1)
    order = jnp.where(order, 1.0, 0.0).astype(jnp.bfloat16)
    ones = jnp.where(chosen, 1.0, 0.0).astype(jnp.bfloat16)
    return jnp.dot(ones, order, preferred_element_type=jnp.float32)


def send_kernel(place_ref, holder_ref, spot_ref, send_ref):
    mine = holder_ref[...] == place_ref[1]
    spot = spot_ref[...].astype(jnp.float32)
    rank = rank_of(mine)
    key = jnp.where(mine & (rank < ROOM), rank, -1.0)
    place_at = iota((HALF, CHUNK), 0).astype(jnp.float32)
    eye = iota((WIDE, WIDE), 0) == iota((WIDE, WIDE), 1)
    depth = iota((CHOICE_DEPTH, WIDE), 0).astype(jnp.float32) + 1.0
    for pair in range(LATS // 2):
        tables = []
        for block in (2 * pair, 2 * pair + 1):
            found = place_at == key[block : block + 1]
            tables.append(
                jnp.sum(jnp.where(found, spot[block : block + 1] + 1.0, 0.0), axis=1, keepdims=True)
            )
        table = jnp.concatenate(tables, axis=0)
        line = jnp.sum(jnp.where(eye, table, 0.0), axis=0, keepdims=True)
        hot = jnp.where(depth == line, 1.0, 0.0).astype(jnp.bfloat16)
        send_ref[:, pair * WIDE : (pair + 1) * WIDE] = hot


def take_kernel(place_ref, holder_ref, take_ref, coef_ref):
    lat = place_ref[1]
    own = holder_ref[pl.ds(lat, 1)]
    masks = iota((PEERS, CHUNK), 0) == own
    rank = jnp.sum(jnp.where(masks, rank_of(masks), 0.0), axis=0, keepdims=True)
    fits = (own >= 0) & (rank < ROOM)
    index = jnp.where(fits, own.astype(jnp.float32) * HALF + rank, -1.0)
    hot = iota((DEPTH, CHUNK), 0).astype(jnp.float32) == index
    take_ref[...] = jnp.where(hot, 1.0, 0.0).astype(jnp.bfloat16)
    row = (lat * ROWS - 8 + iota((TALL, WIDE), 0)).astype(jnp.float32)
    column = (place_ref[2] * COLS - 8 + column_of((TALL, WIDE))).astype(jnp.float32)
    colatitude = 0.25 * math.pi + (row + 0.5) * DTHETA
    longitude = -0.75 * math.pi + (column + 0.5) * DPHI
    sine, cosine = jnp.sin(colatitude), jnp.cos(colatitude)
    twirl = 2.0 * 0.25 / TIME_STEP
    yang = place_ref[0] == 1
    coef_ref[0] = sine
    coef_ref[1] = 1.0 / sine
    coef_ref[2] = twirl * jnp.where(yang, sine * jnp.sin(longitude), cosine)
    coef_ref[3] = twirl * jnp.where(yang, cosine * jnp.sin(longitude), -sine)
    coef_ref[4] = twirl * jnp.where(yang, jnp.cos(longitude), 0.0)


def widen_kernel(place_ref, got_ref, send_ref, lower_ref, west_ref, out_ref, edge_ref):
    column = column_of((8, WIDE))
    for pair in range(PAIRS):
        group, which = pair // 8, pair % 8
        west = turn(west_ref[group, 8:16], -8 * which)
        edge_ref[pair] = jnp.where(column < 8, west, lower_ref[pair, 8:16])
    choice_kernel(place_ref, got_ref, send_ref, out_ref)


def choice_kernel(place_ref, got_ref, send_ref, out_ref):
    parts = from_row(place_ref, got_ref)
    terms = jnp.dot(parts, send_ref[...], preferred_element_type=jnp.float32)
    chosen = join_parts(terms)
    low = iota((16, WIDE), 1) < HALF
    for pair in range(PEERS // 2):
        tile = chosen[:, pair * WIDE : (pair + 1) * WIDE]
        top, end = tile[:16], tile[16:]
        out_ref[2 * pair] = jnp.where(low, top, pltpu.roll(end, HALF, 1))
        out_ref[2 * pair + 1] = jnp.where(low, pltpu.roll(top, HALF, 1), end)


def dense_kernel(place_ref, got_ref, holder_ref, spot_ref, out_ref):
    parts = from_row(place_ref, got_ref)
    index = jnp.where(holder_ref[...] == place_ref[1], spot_ref[...], -1)
    at = iota((CHOICE_DEPTH, CHUNK), 0)
    for block in range(LATS):
        hot = jnp.where(at == index[block : block + 1], 1.0, 0.0).astype(jnp.bfloat16)
        out_ref[block] = join_parts(jnp.dot(parts, hot, preferred_element_type=jnp.float32))


def ghost_values(got_ref, take_ref):
    if len(got_ref.shape) == 2:
        return got_ref[...]
    low = iota((16, WIDE), 1) < HALF
    tiles = []
    for pair in range(PEERS // 2):
        one = got_ref[2 * pair]
        two = got_ref[2 * pair + 1]
        top = jnp.where(low, one, pltpu.roll(two, HALF, 1))
        end = jnp.where(low, pltpu.roll(one, HALF, 1), two)
        tiles.append(jnp.concatenate([top, end], axis=0))
    parts = split_parts(jnp.concatenate(tiles, axis=1))
    return join_parts(jnp.dot(parts, take_ref[...], preferred_element_type=jnp.float32))


def fill_ghosts(place_ref, ghosts, work_ref, rows):
    lat, lon = place_ref[1], place_ref[2]
    trim = (TALL - rows) // 2
    top = 8 - trim
    half = PLANES // 2

    @pl.when((lon == 0) | (lon == LONS - 1))
    def _():
        side = ghosts[:, BAND:]
        first = jnp.where(lon == 0, 4, 8 + COLS)
        own = iota((rows, WIDE), 1) // 4 == iota((rows, WIDE), 0) + trim

        def spread(part):
            return jnp.where(own[None], part[:, None, :], 0.0).reshape(PAIRS * rows, WIDE)

        both = jnp.concatenate([spread(side[:half]), spread(side[half:])], axis=1)
        source = iota((2 * WIDE, WIDE), 0)
        target = first + (source & 3) + jnp.where(source >= WIDE, HALF, 0)
        hot = jnp.where(target == iota((2 * WIDE, WIDE), 1), 1.0, 0.0).astype(jnp.bfloat16)
        moved = split_dot(both, hot).reshape(PAIRS, rows, WIDE)
        column = column_of((rows, WIDE))
        ghost = (column >= first) & (column < first + 4)
        work_ref[...] = jnp.where(ghost[None], moved, work_ref[...])

    @pl.when((lat == 0) | (lat == LATS - 1))
    def _():
        low = iota((half, WIDE), 1) < HALF
        lines = []
        for which in range(2):
            piece = ghosts[:, which * WIDE : (which + 1) * WIDE]
            one, two = piece[:half], piece[half:]
            lines.append(jnp.where(low, one, pltpu.roll(two, HALF, 1)))
            lines.append(jnp.where(low, pltpu.roll(one, HALF, 1), two))

        @pl.when(lat == 0)
        def _():
            for row in range(4):
                work_ref[:, top - 4 + row, :] = lines[row]

        @pl.when(lat == LATS - 1)
        def _():
            for row in range(4):
                work_ref[:, top + ROWS + row, :] = lines[row]


def rates(load, rows, coef_ref, diffusion_ref):
    low = iota((rows, WIDE), 1) < HALF

    def levels(values):
        halves = [
            jnp.where(low, values[LOW_LEVEL[k]], values[HIGH_LEVEL[k]]).astype(jnp.float32)
            for k in range(2)
        ]
        return jnp.concatenate(halves, axis=0)

    def whole(which):
        value = coef_ref[which]
        if rows < TALL:
            value = pltpu.roll(value, TALL - (TALL - rows) // 2, 0)[:rows]
        return jnp.concatenate([value] * 2, axis=0)

    sine = whole(0)
    per_sine = whole(1)
    radius = levels(RADII)
    inverse = levels([1.0 / r for r in RADII])
    square = levels([r * r for r in RADII])
    per_square = levels([1.0 / (r * r) for r in RADII])
    sign = jnp.where(low, 1.0, -1.0)
    ends = sign * (1.0 / RADIAL_STEP)
    inner = sign * (1.0 / (2.0 * RADIAL_STEP))
    viscosity = diffusion_ref[0] * (FINEST * FINEST / TIME_STEP)
    resistivity = diffusion_ref[1] * (FINEST * FINEST / TIME_STEP)

    def slope(value, axis, step):
        size = value.shape[axis]
        near = pltpu.roll(value, size - 1, axis) - pltpu.roll(value, 1, axis)
        far = pltpu.roll(value, size - 2, axis) - pltpu.roll(value, 2, axis)
        return near * (8.0 / (12.0 * step)) - far * (1.0 / (12.0 * step))

    def d_theta(value):
        return slope(value, 0, DTHETA)

    def d_phi(value):
        return slope(value, 1, DPHI)

    def d_radius(value):
        one, two = value[:rows], value[rows:]
        return jnp.concatenate(
            [(two - one) * ends, (pltpu.roll(two, HALF, 1) - one) * inner], axis=0
        )

    def by_radius(value):
        return value * radius

    def per_radius(value):
        return value * inverse

    def curl(vector):
        part_r, part_t, part_p = vector
        return (
            per_radius((d_theta(sine * part_p) - d_phi(part_t)) * per_sine),
            per_radius(d_phi(part_r) * per_sine - d_radius(by_radius(part_p))),
            per_radius(d_radius(by_radius(part_t)) - d_theta(part_r)),
        )

    def gradient(value):
        return (
            d_radius(value),
            per_radius(d_theta(value)),
            per_radius(d_phi(value) * per_sine),
        )

    def cross(left, right):
        return (
            left[1] * right[2] - left[2] * right[1],
            left[2] * right[0] - left[0] * right[2],
            left[0] * right[1] - left[1] * right[0],
        )

    def advect(vector, slopes):
        return vector[0] * slopes[0] + vector[1] * slopes[1] + vector[2] * slopes[2]

    velocity = [load(which) for which in (1, 2, 3)]
    magnetic = [load(which) for which in (4, 5, 6)]
    vorticity = curl(velocity)
    current = curl(magnetic)
    spread = d_radius(square * velocity[0]) * per_square + per_radius(
        (d_theta(sine * velocity[1]) + d_phi(velocity[2])) * per_sine
    )
    induced = cross(velocity, magnetic)
    electric = [induced[k] - resistivity * current[k] for k in range(3)]
    kinetic = 0.5 * (
        velocity[0] * velocity[0] + velocity[1] * velocity[1] + velocity[2] * velocity[2]
    )
    curl_electric = curl(electric)
    log_rho = load(0)
    rho_rate = -advect(velocity, gradient(log_rho)) - spread
    pressure = load(7)
    slope_pressure = gradient(pressure)
    pressure_rate = -advect(velocity, slope_pressure) - GAMMA * pressure * spread
    lorentz = cross(current, magnetic)
    per_rho = jnp.exp(-log_rho)
    slope_kinetic = gradient(kinetic)
    curl_vorticity = curl(vorticity)
    lamb = cross(velocity, vorticity)
    turning = cross((whole(2), whole(3), whole(4)), velocity)
    momentum = [
        lamb[k]
        - slope_kinetic[k]
        + per_rho * (lorentz[k] - slope_pressure[k])
        - turning[k]
        - viscosity * curl_vorticity[k]
        for k in range(3)
    ]
    return [rho_rate, *momentum, *curl_electric, pressure_rate]


def first_kernel(
    place_ref,
    diffusion_ref,
    lower_ref,
    north_ref,
    west_ref,
    got_ref,
    take_ref,
    coef_ref,
    pick_ref,
    mix_ref,
    spin_ref,
    flag_ref,
    middle_ref,
    out_ref,
    work_ref,
    next_ref,
):
    column = column_of((TALL, WIDE))
    for pair in range(PAIRS):
        group, which = pair // 8, pair % 8
        west = turn(west_ref[group], -8 * which)
        work_ref[pair, :8] = north_ref[pair]
        work_ref[pair, 8:] = jnp.where(column[8:] < 8, west, lower_ref[pair])
    ghosts = ghost_values(got_ref, take_ref)
    fill_ghosts(place_ref, ghosts, work_ref, TALL)

    def load(which):
        return work_ref[2 * which : 2 * which + 2].reshape(2 * TALL, WIDE)

    found = rates(load, TALL, coef_ref, diffusion_ref)
    row = iota((TALL, WIDE), 0)
    inside = (column >= 4) & (column < 12 + COLS) & (row >= 4) & (row < 12 + ROWS)
    for which in range(FIELDS):
        value = load(which) + (0.5 * TIME_STEP) * found[which]
        for half in range(2):
            part = jnp.where(inside, value[half * TALL : (half + 1) * TALL], 0.0)
            next_ref[2 * which + half] = part[8:]
            middle_ref[2 * which + half] = pltpu.roll(part, TALL - 4, 0)[:MID]
    planes = next_ref[...].reshape(PAIRS * MID, WIDE)
    packed = donor_message(planes, pick_ref[...], mix_ref[...], spin_ref[...])
    post_message(place_ref, packed, flag_ref[0:1], out_ref)


def second_kernel(
    place_ref,
    diffusion_ref,
    middle_ref,
    got_ref,
    take_ref,
    coef_ref,
    held_ref,
    whole_ref,
    third_ref,
    work_ref,
):
    work_ref[...] = middle_ref[...]
    ghosts = ghost_values(got_ref, take_ref)
    fill_ghosts(place_ref, ghosts, work_ref, MID)

    def load(which):
        return work_ref[2 * which : 2 * which + 2].reshape(2 * MID, WIDE)

    found = rates(load, MID, coef_ref, diffusion_ref)

    def centre(value):
        return pltpu.roll(value, MID - 4, 0)[:ROWS]

    def place(out_ref, pair, value):
        field, half = pair // 2, pair % 2
        out_ref[field, LOW_LEVEL[half]] = turn(value, -8)[:, :COLS]
        out_ref[field, HIGH_LEVEL[half]] = turn(value, -8 - HALF)[:, :COLS]

    for pair in range(PAIRS):
        field, half = pair // 2, pair % 2
        rate = found[field][half * MID : (half + 1) * MID]
        held = held_ref[pair]
        step = centre(rate) * (0.5 * TIME_STEP)
        middle = centre(middle_ref[pair])
        place(third_ref, pair, held + step)
        place(whole_ref, pair, held + ((middle - held) + 2.0 * step) * (1.0 / 3.0))


def shift(value, move_lat, move_lon):
    pairs = []
    for a in range(LATS):
        for b in range(LONS):
            goal_a, goal_b = a + move_lat, b + move_lon
            if 0 <= goal_a < LATS and 0 <= goal_b < LONS:
                pairs.append((a * LONS + b, goal_a * LONS + goal_b))
    return lax.ppermute(value, ("lat", "lon"), pairs)


def shards(state, donor_cell, donor_weights, donor_turn, border_source, diffusion):
    fields = state[0]
    panel = lax.axis_index("panel")
    lat = lax.axis_index("lat")
    lon = lax.axis_index("lon")
    place = jnp.stack([panel, lat, lon]).astype(jnp.int32)
    f32 = jnp.float32

    def call(kernel, outs, *args, smem=0, specs=None, scratch=(), limit=10):
        shapes = [jax.ShapeDtypeStruct(shape, dtype) for shape, dtype in outs]
        return pl.pallas_call(
            kernel,
            out_shape=shapes,
            in_specs=specs or [SMEM] * smem + [VMEM] * (len(args) - smem),
            out_specs=[VMEM] * len(outs),
            scratch_shapes=scratch,
            compiler_params=pltpu.CompilerParams(vmem_limit_bytes=limit * MIB),
        )(*args)

    bf16 = jnp.bfloat16
    held, south, east, corner = call(
        cut_kernel,
        [
            ((PAIRS, ROWS, WIDE), f32),
            ((PAIRS, 8, WIDE), f32),
            ((2, ROWS, WIDE), f32),
            ((2, 8, WIDE), f32),
        ],
        fields,
        scratch=[pltpu.VMEM((PLANES, ROWS, WIDE), f32)],
    )
    south = shift(south, -1, 0)
    east = shift(east, 0, -1)
    corner = shift(corner, -1, -1)

    donor = jnp.concatenate(
        [donor_cell[0, 0].astype(f32), donor_weights[0, 0, 0], donor_turn[0, 0]], axis=0
    )
    pick, mix, spin = call(
        donor_tables,
        [((WIDE, 2 * WIDE), bf16), ((MID, 2 * WIDE), f32), ((2, WIDE), f32)],
        donor,
        scratch=[pltpu.VMEM((1, WIDE), f32)],
    )
    message = ((2 * PEERS, 1, MESSAGE), f32)
    lower, sent = call(
        donor_kernel,
        [((PAIRS, MID, WIDE), f32), message],
        place,
        held,
        south,
        east,
        corner,
        pick,
        mix,
        spin,
        smem=1,
    )

    def to_holders(sent):
        return lax.all_to_all(sent, ("panel", "lon"), 0, 0, tiled=True)

    got = to_holders(sent)

    late_lat, late_lon, border, late_lower, _ = lax.optimization_barrier(
        (lat, lon, border_source[0], lower, sent)
    )
    (west,) = call(last_kernel, [((2, MID, WIDE), f32)], late_lower)
    west = shift(west, 0, 1)

    ring = PANEL_COLS + 8
    row_slots = LONS * SLOTS
    bands = border[: 8 * ring].reshape(8, ring)
    sides = border[8 * ring :].reshape(PANEL_ROWS, 8)
    window = jnp.pad(bands, ((0, 0), (4, 4)), constant_values=-1)
    window = lax.dynamic_slice(window, (0, late_lon * COLS), (8, 64)).reshape(2, BAND)
    side = jnp.where(late_lon == 0, sides[:, :4], sides[:, 4:])
    side = jnp.where((late_lon == 0) | (late_lon == LONS - 1), side, -1)
    side = jnp.pad(side, ((8, 8), (0, 0)), constant_values=-1)
    side = jnp.concatenate(
        [
            side[:PANEL_ROWS].reshape(LATS, ROWS, 4),
            side[ROWS:].reshape(LATS, ROWS, 4),
        ],
        axis=1,
    ).reshape(LATS, SIDE)
    at_lat = jnp.arange(LATS)[:, None]
    band = jnp.where(at_lat == 0, window[:1], jnp.where(at_lat == LATS - 1, window[1:], -1))
    wanted = jnp.concatenate([band, side], axis=1)
    holder = jnp.where(wanted >= 0, wanted // row_slots, -1)
    local = wanted - late_lat * row_slots
    block = local // SLOTS
    slot = local % SLOTS
    spot = jnp.where(slot < PACKED, block * PACKED + slot, PEERS * PACKED + block)
    (send,) = call(
        send_kernel, [((CHOICE_DEPTH, DEPTH), bf16)], place, holder, spot, smem=1, limit=16
    )
    chunk = ((PEERS, 16, WIDE), f32)
    first_got = got
    chunks, north = call(
        widen_kernel, [chunk, ((PAIRS, 8, WIDE), f32)], place, got, send, lower, west, smem=1
    )
    north = shift(north, 1, 0)
    late_holder, bands, sides, _ = lax.optimization_barrier((holder, bands, sides, chunks))
    take, coef = call(
        take_kernel,
        [((DEPTH, CHUNK), bf16), ((5, TALL, WIDE), f32)],
        place,
        late_holder,
        smem=1,
    )

    (flag,) = call(
        count_kernel,
        [((8, WIDE), f32)],
        jnp.pad(bands, ((0, 0), (0, 7 * WIDE - ring)), constant_values=-1),
        sides.T,
    )

    def to_blocks(chunks):
        return lax.all_to_all(chunks, "lat", 0, 0, tiled=True)

    def section_one(got):
        return call(
            first_kernel,
            [((PAIRS, MID, WIDE), f32), message],
            place,
            diffusion,
            lower,
            north,
            west,
            got,
            take,
            coef,
            pick,
            mix,
            spin,
            flag,
            smem=2,
            scratch=[pltpu.VMEM((PAIRS, TALL, WIDE), f32), pltpu.VMEM((PAIRS, MID, WIDE), f32)],
        )

    def section_two(middle, got):
        return call(
            second_kernel,
            [(fields.shape, f32), (fields.shape, f32)],
            place,
            diffusion,
            middle,
            got,
            take,
            coef,
            held,
            smem=2,
            scratch=[pltpu.VMEM((PAIRS, MID, WIDE), f32)],
        )

    middle, sent = section_one(to_blocks(chunks))
    got = to_holders(sent)
    crowded = jnp.maximum(got[0, 0, FLAG], got[PEERS, 0, FLAG]) > ROOM
    (chunks,) = call(choice_kernel, [chunk], place, got, send, smem=1)
    fitting = section_two(middle, to_blocks(chunks))

    def with_room():
        def dense(got):
            chunks = call(
                dense_kernel,
                [((PEERS, PLANES, CHUNK), f32)],
                place,
                got,
                holder,
                spot,
                smem=1,
                limit=16,
            )
            return to_blocks(chunks[0]).sum(axis=0)

        middle, sent = section_one(dense(first_got))
        return section_two(middle, dense(to_holders(sent)))

    accumulated, section_three = lax.cond(crowded, with_room, lambda: fitting)
    return (accumulated[None], section_three[None])


def solution(mesh):
    return jax.shard_map(
        shards,
        mesh=mesh,
        in_specs=(
            P("panel", None, None, "lat", "lon"),
            P("panel", "lat", "lon", None),
            P("panel", "lat", "lon", None, None),
            P("panel", "lat", "lon", None),
            P("panel", None),
            P(),
        ),
        out_specs=(P("panel", None, None, "lat", "lon"), P("panel", None, None, "lat", "lon")),
        check_vma=False,
    )
```

profile of v0, /device:TPU:1, one launch (start us, length us, event | category | flops | bytes accessed | tf_op | source)
XLA Modules:
  0.0 93.3 jit_solution(10503801265693951597)
XLA Ops:
  0.6 0.9 %copy-done = f32[1,8,4,16,48]{4,3,2,1,0:T(8,128)S(1)} copy-done((f32[1,8,4,16,48]{4,3,2,1,0:T(8,128)S(1)}, f32[1,8,4,16,48]{4,3,2,1,0:T(8,128)}, u32[]{:S(2)}) %copy-start) | copy-done | bytes 98328
  1.8 1.3 %collective-permute-start.2 = (f32[2,8,128]{2,1,0:T(8,128)S(1)}, f32[2,8,128]{2,1,0:T(8,128)S(1)}, u32[]{:S(2)}, u32[]{:S(2)}) collective-permute-start(f32[2,8,128]{2,1,0:T(8,128)S(1)} %get-tuple-element.88), channel_id=1, source_target_pairs={{17,0},{18,1},{19,2},{20,3},{21,4},{22,5},{23,6},{24,7},{25,8},{26... | collective-permute-start | bytes 24584 | tf_op jit(solution)/shard_map/ppermute | solution.py:592
  3.1 1.3 %collective-permute-start.1 = (f32[2,16,128]{2,1,0:T(8,128)S(1)}, f32[2,16,128]{2,1,0:T(8,128)S(1)}, u32[]{:S(2)}, u32[]{:S(2)}) collective-permute-start(f32[2,16,128]{2,1,0:T(8,128)S(1)} %get-tuple-element.87), channel_id=1, source_target_pairs={{1,0},{2,1},{3,2},{4,3},{5,4},{6,5},{7,6},{8,7},{9,8},{10,9},{11,1... | collective-permute-start | bytes 49160 | tf_op jit(solution)/shard_map/ppermute | solution.py:592
  4.4 8.8 %collective-permute-start = (f32[16,8,128]{2,1,0:T(8,128)S(1)}, f32[16,8,128]{2,1,0:T(8,128)S(1)}, u32[]{:S(2)}, u32[]{:S(2)}) collective-permute-start(f32[16,8,128]{2,1,0:T(8,128)S(1)} %get-tuple-element.86), channel_id=1, source_target_pairs={{16,0},{17,1},{18,2},{19,3},{20,4},{21,5},{22,6},{23,7},{24,8},{25... | collective-permute-start | bytes 196616 | tf_op jit(solution)/shard_map/ppermute | solution.py:592
  13.2 0.7 convert_bitcast_fusion
  13.9 0.7 pad_maximum_fusion.donor_ref
  14.8 0.8 reduce
  15.7 1.8 %shard_map.79 = (f32[16,24,128]{2,1,0:T(8,128)S(1)}, f32[32,1,1152]{2,1,0:T(1,128)}) custom-call(s32[3]{0:T(128)S(1)} %pad_add_fusion.2.place_ref, f32[16,16,128]{2,1,0:T(8,128)S(1)} %get-tuple-element.85.held_ref, f32[16,8,128]{2,1,0:T(8,128)S(1)} %collective-permute-done.south_ref, f32[2,16,128]{2,1,0:T(8,128)S(1)} %collective-permute-done.1.east_ref, ...), custom_call_target="tpu_custom_call" | custom-call | tf_op jit(solution)/shard_map/pallas_call | solution.py:605
  17.5 7.5 %all-to-all-start.3 = ((f32[32,1,1152]{2,1,0:T(1,128)}), f32[32,1,1152]{2,1,0:T(1,128)S(1)}, u32[]{:S(2)}, u32[]{:S(2)}) async-start(f32[32,1,1152]{2,1,0:T(1,128)} %get-tuple-element.93), calls=%async_computation.3 | async-start | bytes 294912 | tf_op jit(solution)/shard_map/all_to_all | solution.py:655
  25.5 3.1 %collective-permute-start.3 = (f32[2,24,128]{2,1,0:T(8,128)S(1)}, f32[2,24,128]{2,1,0:T(8,128)S(1)}, u32[]{:S(2)}, u32[]{:S(2)}) collective-permute-start(f32[2,24,128]{2,1,0:T(8,128)S(1)} %shard_map.81), channel_id=1, source_target_pairs={{0,1},{1,2},{2,3},{3,4},{4,5},{5,6},{6,7},{7,8},{8,9},{9,10},{10,1... | collective-permute-start | bytes 73736 | tf_op jit(solution)/shard_map/ppermute | solution.py:592
  29.5 1.8 %shard_map.80.send_ref = bf16[640,1024]{1,0:T(8,128)(2,1)S(1)} custom-call(s32[3]{0:T(128)S(1)} %pad_add_fusion.2.place_ref, s32[16,384]{1,0:T(8,128)S(1)} %get-tuple-element.100.holder_ref, s32[16,384]{1,0:T(8,128)S(1)} %get-tuple-element.119.spot_ref), custom_call_target="tpu_custom_call" | custom-call | tf_op jit(solution)/shard_map/pallas_call | solution.py:605
  31.3 3.1 %all-to-all-done.3.got_ref = f32[32,1,1152]{2,1,0:T(1,128)S(1)} async-done(((f32[32,1,1152]{2,1,0:T(1,128)}), f32[32,1,1152]{2,1,0:T(1,128)S(1)}, u32[]{:S(2)}, u32[]{:S(2)}) %all-to-all-start.3) | async-done | bytes 147488 | tf_op jit(solution)/shard_map/all_to_all | solution.py:655
  34.4 1.7 %shard_map.82 = (f32[16,16,128]{2,1,0:T(8,128)}, f32[16,8,128]{2,1,0:T(8,128)S(1)}) custom-call(s32[3]{0:T(128)S(1)} %pad_add_fusion.2.place_ref, f32[32,1,1152]{2,1,0:T(1,128)S(1)} %all-to-all-done.3.got_ref, bf16[640,1024]{1,0:T(8,128)(2,1)S(1)} %shard_map.80.send_ref, f32[16,24,128]{2,1,0:T(8,128)S(1)} %get-tuple-element.97.lower_ref, ...), custom_call_target="tpu_custom_call" | custom-call | tf_op jit(solution)/shard_map/pallas_call | solution.py:605
  36.1 11.4 %all-to-all-start.4 = ((f32[16,16,128]{2,1,0:T(8,128)}), f32[16,16,128]{2,1,0:T(8,128)S(1)}, u32[]{:S(2)}, u32[]{:S(2)}) async-start(f32[16,16,128]{2,1,0:T(8,128)} %get-tuple-element.99), calls=%async_computation.4 | async-start | bytes 262144 | tf_op jit(solution)/shard_map/all_to_all | solution.py:715
  47.6 3.5 %collective-permute-start.4 = (f32[16,8,128]{2,1,0:T(8,128)S(1)}, f32[16,8,128]{2,1,0:T(8,128)S(1)}, u32[]{:S(2)}, u32[]{:S(2)}) collective-permute-start(f32[16,8,128]{2,1,0:T(8,128)S(1)} %get-tuple-element.98), channel_id=1, source_target_pairs={{0,16},{1,17},{2,18},{3,19},{4,20},{5,21},{6,22},{7,23},{8,24},{9,... | collective-permute-start | bytes 196616 | tf_op jit(solution)/shard_map/ppermute | solution.py:592
  51.1 1.0 %shard_map.83 = (bf16[1024,384]{1,0:T(8,128)(2,1)S(1)}, f32[5,32,128]{2,1,0:T(8,128)S(1)}) custom-call(s32[3]{0:T(128)S(1)} %pad_add_fusion.2.place_ref, s32[16,384]{1,0:T(8,128)S(1)} %get-tuple-element.100.holder_ref), custom_call_target="tpu_custom_call" | custom-call | tf_op jit(solution)/shard_map/pallas_call | solution.py:605
  52.8 4.0 %all-to-all-done.4.got_ref = f32[16,16,128]{2,1,0:T(8,128)S(1)} async-done(((f32[16,16,128]{2,1,0:T(8,128)}), f32[16,16,128]{2,1,0:T(8,128)S(1)}, u32[]{:S(2)}, u32[]{:S(2)}) %all-to-all-start.4) | async-done | bytes 131104 | tf_op jit(solution)/shard_map/all_to_all | solution.py:715
  56.8 2.2 %shard_map.85 = (f32[16,24,128]{2,1,0:T(8,128)S(1)}, f32[32,1,1152]{2,1,0:T(1,128)S(1)}) custom-call(s32[3]{0:T(128)S(1)} %pad_add_fusion.2.place_ref, f32[2]{0:T(128)S(1)} %copy-done.1, f32[16,24,128]{2,1,0:T(8,128)S(1)} %get-tuple-element.97.lower_ref, f32[16,8,128]{2,1,0:T(8,128)S(1)} %collective-permute-done.4.north_ref, ...), custom_call_target="tpu_custom_call" | custom-call | tf_op jit(solution)/shard_map/pallas_call | solution.py:605
  59.0 14.7 %all_to_all.35.got_ref = f32[32,1,1152]{2,1,0:T(1,128)S(1)} all-to-all(f32[32,1,1152]{2,1,0:T(1,128)S(1)} %get-tuple-element.105), channel_id=1, replica_groups=mesh['panel'=2,'lat'=16,'lon'=16] {'panel','lon'}, dimensions={0} | all-to-all | bytes 294912 | tf_op jit(solution)/shard_map/all_to_all | solution.py:655
  73.7 1.7 %shard_map.86 = f32[16,16,128]{2,1,0:T(8,128)} custom-call(s32[3]{0:T(128)S(1)} %pad_add_fusion.2.place_ref, f32[32,1,1152]{2,1,0:T(1,128)S(1)} %all_to_all.35.got_ref, bf16[640,1024]{1,0:T(8,128)(2,1)S(1)} %shard_map.80.send_ref), custom_call_target="tpu_custom_call" | custom-call | tf_op jit(solution)/shard_map/pallas_call | solution.py:605
  75.4 6.0 %all-to-all-start.6 = ((f32[16,16,128]{2,1,0:T(8,128)}), f32[16,16,128]{2,1,0:T(8,128)S(1)}, u32[]{:S(2)}, u32[]{:S(2)}) async-start(f32[16,16,128]{2,1,0:T(8,128)} %shard_map.86), calls=%async_computation.6 | async-start | bytes 262144 | tf_op jit(solution)/shard_map/all_to_all | solution.py:715
  81.4 0.7 fusion.4
  83.5 7.2 %all-to-all-done.6.got_ref = f32[16,16,128]{2,1,0:T(8,128)S(1)} async-done(((f32[16,16,128]{2,1,0:T(8,128)}), f32[16,16,128]{2,1,0:T(8,128)S(1)}, u32[]{:S(2)}, u32[]{:S(2)}) %all-to-all-start.6) | async-done | bytes 131104 | tf_op jit(solution)/shard_map/all_to_all | solution.py:715
  90.6 2.7 %shard_map.87 = (f32[8,4,16,48]{3,2,1,0:T(8,128)}, f32[8,4,16,48]{3,2,1,0:T(8,128)}) custom-call(s32[3]{0:T(128)S(1)} %pad_add_fusion.2.place_ref, f32[2]{0:T(128)S(1)} %copy-done.1, f32[16,24,128]{2,1,0:T(8,128)S(1)} %get-tuple-element.106.middle_ref, f32[16,16,128]{2,1,0:T(8,128)S(1)} %all-to-all-done.6.got_ref, ...), custom_call_target="tpu_custom_call" | custom-call | tf_op jit(solution)/shard_map/pallas_call | solution.py:605
  (33 shorter events, 2.5 us)
Async XLA Ops:
  0.6 1.0 %copy-start = (f32[1,8,4,16,48]{4,3,2,1,0:T(8,128)S(1)}, f32[1,8,4,16,48]{4,3,2,1,0:T(8,128)}, u32[]{:S(2)}) copy-start(f32[1,8,4,16,48]{4,3,2,1,0:T(8,128)} %param.8) | copy-start | bytes 294916
  1.8 13.9 %collective-permute-start.2 = (f32[2,8,128]{2,1,0:T(8,128)S(1)}, f32[2,8,128]{2,1,0:T(8,128)S(1)}, u32[]{:S(2)}, u32[]{:S(2)}) collective-permute-start(f32[2,8,128]{2,1,0:T(8,128)S(1)} %get-tuple-element.88), channel_id=1, source_target_pairs={{17,0},{18,1},{19,2},{20,3},{21,4},{22,5},{23,6},{24,7},{25,8},{26... | collective-permute-start | bytes 24584 | tf_op jit(solution)/shard_map/ppermute | solution.py:592
  3.1 12.6 %collective-permute-start.1 = (f32[2,16,128]{2,1,0:T(8,128)S(1)}, f32[2,16,128]{2,1,0:T(8,128)S(1)}, u32[]{:S(2)}, u32[]{:S(2)}) collective-permute-start(f32[2,16,128]{2,1,0:T(8,128)S(1)} %get-tuple-element.87), channel_id=1, source_target_pairs={{1,0},{2,1},{3,2},{4,3},{5,4},{6,5},{7,6},{8,7},{9,8},{10,9},{11,1... | collective-permute-start | bytes 49160 | tf_op jit(solution)/shard_map/ppermute | solution.py:592
  4.4 11.3 %collective-permute-start = (f32[16,8,128]{2,1,0:T(8,128)S(1)}, f32[16,8,128]{2,1,0:T(8,128)S(1)}, u32[]{:S(2)}, u32[]{:S(2)}) collective-permute-start(f32[16,8,128]{2,1,0:T(8,128)S(1)} %get-tuple-element.86), channel_id=1, source_target_pairs={{16,0},{17,1},{18,2},{19,3},{20,4},{21,5},{22,6},{23,7},{24,8},{25... | collective-permute-start | bytes 196616 | tf_op jit(solution)/shard_map/ppermute | solution.py:592
  17.5 16.9 %all-to-all-start.3 = ((f32[32,1,1152]{2,1,0:T(1,128)}), f32[32,1,1152]{2,1,0:T(1,128)S(1)}, u32[]{:S(2)}, u32[]{:S(2)}) async-start(f32[32,1,1152]{2,1,0:T(1,128)} %get-tuple-element.93), calls=%async_computation.3 | async-start | bytes 294912 | tf_op jit(solution)/shard_map/all_to_all | solution.py:655
  25.5 5.8 %collective-permute-start.3 = (f32[2,24,128]{2,1,0:T(8,128)S(1)}, f32[2,24,128]{2,1,0:T(8,128)S(1)}, u32[]{:S(2)}, u32[]{:S(2)}) collective-permute-start(f32[2,24,128]{2,1,0:T(8,128)S(1)} %shard_map.81), channel_id=1, source_target_pairs={{0,1},{1,2},{2,3},{3,4},{4,5},{5,6},{6,7},{7,8},{8,9},{9,10},{10,1... | collective-permute-start | bytes 73736 | tf_op jit(solution)/shard_map/ppermute | solution.py:592
  31.3 25.5 %copy-start.1 = (f32[2]{0:T(128)S(1)}, f32[2]{0:T(128)}, u32[]{:S(2)}) copy-start(f32[2]{0:T(128)} %diffusion_ref.3) | copy-start | bytes 28
  36.1 20.7 %all-to-all-start.4 = ((f32[16,16,128]{2,1,0:T(8,128)}), f32[16,16,128]{2,1,0:T(8,128)S(1)}, u32[]{:S(2)}, u32[]{:S(2)}) async-start(f32[16,16,128]{2,1,0:T(8,128)} %get-tuple-element.99), calls=%async_computation.4 | async-start | bytes 262144 | tf_op jit(solution)/shard_map/all_to_all | solution.py:715
  47.6 5.3 %collective-permute-start.4 = (f32[16,8,128]{2,1,0:T(8,128)S(1)}, f32[16,8,128]{2,1,0:T(8,128)S(1)}, u32[]{:S(2)}, u32[]{:S(2)}) collective-permute-start(f32[16,8,128]{2,1,0:T(8,128)S(1)} %get-tuple-element.98), channel_id=1, source_target_pairs={{0,16},{1,17},{2,18},{3,19},{4,20},{5,21},{6,22},{7,23},{8,24},{9,... | collective-permute-start | bytes 196616 | tf_op jit(solution)/shard_map/ppermute | solution.py:592
  75.4 15.2 %all-to-all-start.6 = ((f32[16,16,128]{2,1,0:T(8,128)}), f32[16,16,128]{2,1,0:T(8,128)S(1)}, u32[]{:S(2)}, u32[]{:S(2)}) async-start(f32[16,16,128]{2,1,0:T(8,128)} %shard_map.86), calls=%async_computation.6 | async-start | bytes 262144 | tf_op jit(solution)/shard_map/all_to_all | solution.py:715
where the time goes:
time: 93.9 us; the launch traced here: 93.3 us
  starting transfers between devices  43 us (46%)
  blocking collectives  14.7 us (16%)
  waiting for transfers between devices  14.4 us (15%)
  Pallas kernels  13.7 us (15%)
  local copies, waits for them, and re-layouts  2.62 us (3%)
  other arithmetic  2.55 us (3%)
  between operations  2.21 us (2%)
    ppermute x5, starting transfers between devices, shift(): return lax.ppermute(value, ('lat', 'lon'), pairs)  18 us
    all_to_all x2, starting transfers between devices, to_blocks(): return lax.all_to_all(chunks, 'lat', 0, 0, tiled=True)  17.5 us
    all_to_all x1, blocking collectives, to_holders(): return lax.all_to_all(sent, ('panel', 'lon'), 0, 0, tiled=True)  14.7 us
    pallas_call x11, Pallas kernels, call(): pl.pallas_call(kernel, out_shape=shapes, in_specs=specs or [SMEM] * smem...  13.7 us
    all_to_all x2, waiting for transfers between devices, to_blocks(): return lax.all_to_all(chunks, 'lat', 0, 0, tiled=True)  11.1 us
    all_to_all x1, starting transfers between devices, to_holders(): return lax.all_to_all(sent, ('panel', 'lon'), 0, 0, tiled=True)  7.52 us
    all_to_all x1, waiting for transfers between devices, to_holders(): return lax.all_to_all(sent, ('panel', 'lon'), 0, 0, tiled=True)  3.11 us
  transfers between devices with their start and end apart: 8, of which 4 were waited for; matrix products, arithmetic and copies ran while one was open for 4% of the time, Pallas kernels for 4%

commit v1 on v0

--- a/solution.py
+++ b/solution.py
@@ -60,18 +60,19 @@
     return pltpu.roll(value, lanes % WIDE, 1) if lanes % WIDE else value
 
 
-def split_dot(left, right):
-    total = None
+def three_parts(value):
+    parts = []
     for _ in range(3):
-        part = left.astype(jnp.bfloat16)
-        left = left - part.astype(jnp.float32)
-        term = jnp.dot(part, right, preferred_element_type=jnp.float32)
-        total = term if total is None else total + term
-    return total
+        part = value.astype(jnp.bfloat16)
+        value = value - part.astype(jnp.float32)
+        parts.append(part)
+    return parts
 
 
 def donor_message(planes, pick, mix, spin):
-    chosen = split_dot(planes, pick).reshape(PAIRS, MID, 2 * WIDE)
+    parts = jnp.concatenate(three_parts(planes), axis=1)
+    chosen = jnp.dot(parts, pick, preferred_element_type=jnp.float32)
+    chosen = chosen.reshape(PAIRS, MID, 2 * WIDE)
     both = jnp.sum(chosen * mix[None], axis=1)
     both = jnp.concatenate([both[:, :WIDE], both[:, WIDE:]], axis=0)
     mixed = both + pltpu.roll(both, HALF, 1)
@@ -150,8 +151,11 @@
     spin_ref[1:2] = jnp.sin(angle)
     lane = iota((WIDE, WIDE), 0).astype(jnp.float32)
     real = jnp.where(row_at >= 0, col_at + 8.0, -1000.0)
-    pick_ref[:, :WIDE] = jnp.where(lane == real, 1.0, 0.0).astype(jnp.bfloat16)
-    pick_ref[:, WIDE:] = jnp.where(lane == real + HALF, 1.0, 0.0).astype(jnp.bfloat16)
+    low = jnp.where(lane == real, 1.0, 0.0).astype(jnp.bfloat16)
+    high = jnp.where(lane == real + HALF, 1.0, 0.0).astype(jnp.bfloat16)
+    for part in range(3):
+        pick_ref[part * WIDE : (part + 1) * WIDE, :WIDE] = low
+        pick_ref[part * WIDE : (part + 1) * WIDE, WIDE:] = high
     row = iota((MID, WIDE), 0).astype(jnp.float32)
     mix = jnp.where(row == row_at, upper, 0.0) + jnp.where(row == row_at + 1.0, lower, 0.0)
     mix_ref[:, :WIDE] = mix
@@ -211,12 +215,7 @@
 
 
 def split_parts(held):
-    parts = []
-    for _ in range(3):
-        part = held.astype(jnp.bfloat16)
-        held = held - part.astype(jnp.float32)
-        parts.append(part)
-    return jnp.concatenate(parts, axis=0)
+    return jnp.concatenate(three_parts(held), axis=0)
 
 
 def join_parts(terms):
@@ -355,13 +354,18 @@
         own = iota((rows, WIDE), 1) // 4 == iota((rows, WIDE), 0) + trim
 
         def spread(part):
-            return jnp.where(own[None], part[:, None, :], 0.0).reshape(PAIRS * rows, WIDE)
-
-        both = jnp.concatenate([spread(side[:half]), spread(side[half:])], axis=1)
-        source = iota((2 * WIDE, WIDE), 0)
-        target = first + (source & 3) + jnp.where(source >= WIDE, HALF, 0)
-        hot = jnp.where(target == iota((2 * WIDE, WIDE), 1), 1.0, 0.0).astype(jnp.bfloat16)
-        moved = split_dot(both, hot).reshape(PAIRS, rows, WIDE)
+            part = part.astype(jnp.float32)[:, None, :]
+            return jnp.where(own[None], part, 0.0).astype(jnp.bfloat16).reshape(PAIRS * rows, WIDE)
+
+        pieces = []
+        for part in three_parts(side):
+            pieces += [spread(part[:half]), spread(part[half:])]
+        both = jnp.concatenate(pieces, axis=1)
+        source = iota((6 * WIDE, WIDE), 0)
+        target = first + (source & 3) + jnp.where((source & WIDE) != 0, HALF, 0)
+        hot = jnp.where(target == iota((6 * WIDE, WIDE), 1), 1.0, 0.0).astype(jnp.bfloat16)
+        moved = jnp.dot(both, hot, preferred_element_type=jnp.float32)
+        moved = moved.reshape(PAIRS, rows, WIDE)
         column = column_of((rows, WIDE))
         ghost = (column >= first) & (column < first + 4)
         work_ref[...] = jnp.where(ghost[None], moved, work_ref[...])
@@ -632,7 +636,7 @@
     )
     pick, mix, spin = call(
         donor_tables,
-        [((WIDE, 2 * WIDE), bf16), ((MID, 2 * WIDE), f32), ((2, WIDE), f32)],
+        [((3 * WIDE, 2 * WIDE), bf16), ((MID, 2 * WIDE), f32), ((2, WIDE), f32)],
         donor,
         scratch=[pltpu.VMEM((1, WIDE), f32)],
     )
@@ -657,8 +661,9 @@
     got = to_holders(sent)
 
     late_lat, late_lon, border, late_lower, _ = lax.optimization_barrier(
-        (lat, lon, border_source[0], lower, sent)
-    )
+        (lat, lon, border_source, lower, sent)
+    )
+    border = border[0]
     (west,) = call(last_kernel, [((2, MID, WIDE), f32)], late_lower)
     west = shift(west, 0, 1)
 

time: 93.9 us -> 94.9 us (1.011)
  blocking collectives: 14.7 us -> 16.5 us
  local copies, waits for them, and re-layouts: 2.62 us -> 4.07 us
    all_to_all x1, blocking collectives: 14.7 us -> 16.5 us  [to_holders(): return lax.all_to_all(sent, ('panel', 'lon'), 0, 0, tiled=True)]
    all_to_all x1, waiting for transfers between devices: 3.11 us -> 1.57 us  [to_holders(): return lax.all_to_all(sent, ('panel', 'lon'), 0, 0, tiled=True)]
  transfers between devices with their start and end apart: 8 -> 8, of which waited for: 4 -> 5; matrix products, arithmetic and copies ran while one was open for 4% -> 5% of each run, Pallas kernels for 4% -> 4%
where the time goes in v1:
time: 94.9 us; the launch traced here: 94.3 us
  starting transfers between devices  42.6 us (45%)
  blocking collectives  16.5 us (17%)
  Pallas kernels  13.7 us (14%)
  waiting for transfers between devices  13.5 us (14%)
  local copies, waits for them, and re-layouts  4.07 us (4%)
  between operations  2.15 us (2%)
  other arithmetic  1.71 us (2%)
    ppermute x5, starting transfers between devices, shift(): return lax.ppermute(value, ('lat', 'lon'), pairs)  18 us
    all_to_all x2, starting transfers between devices, to_blocks(): return lax.all_to_all(chunks, 'lat', 0, 0, tiled=True)  16.7 us
    all_to_all x1, blocking collectives, to_holders(): return lax.all_to_all(sent, ('panel', 'lon'), 0, 0, tiled=True)  16.5 us
    pallas_call x11, Pallas kernels, call(): pl.pallas_call(kernel, out_shape=shapes, in_specs=specs or [SMEM] * smem...  13.7 us
    all_to_all x2, waiting for transfers between devices, to_blocks(): return lax.all_to_all(chunks, 'lat', 0, 0, tiled=True)  11.2 us
    all_to_all x1, starting transfers between devices, to_holders(): return lax.all_to_all(sent, ('panel', 'lon'), 0, 0, tiled=True)  7.87 us
  transfers between devices with their start and end apart: 8, of which 5 were waited for; matrix products, arithmetic and copies ran while one was open for 5% of the time, Pallas kernels for 4%

profile of v1, /device:TPU:1, one launch (start us, length us, event | category | flops | bytes accessed | tf_op | source)
XLA Modules:
  0.0 94.3 jit_solution(10649733946977674726)
XLA Ops:
  0.6 0.9 copy-done
  1.8 1.3 %collective-permute-start.2 = (f32[2,8,128]{2,1,0:T(8,128)S(1)}, f32[2,8,128]{2,1,0:T(8,128)S(1)}, u32[]{:S(2)}, u32[]{:S(2)}) collective-permute-start(f32[2,8,128]{2,1,0:T(8,128)S(1)} %get-tuple-element.88), channel_id=1, source_target_pairs={{17,0},{18,1},{19,2},{20,3},{21,4},{22,5},{23,6},{24,7},{25,8},{26... | collective-permute-start | bytes 24584 | tf_op jit(solution)/shard_map/ppermute | solution.py:596
  3.1 1.3 %collective-permute-start.1 = (f32[2,16,128]{2,1,0:T(8,128)S(1)}, f32[2,16,128]{2,1,0:T(8,128)S(1)}, u32[]{:S(2)}, u32[]{:S(2)}) collective-permute-start(f32[2,16,128]{2,1,0:T(8,128)S(1)} %get-tuple-element.87), channel_id=1, source_target_pairs={{1,0},{2,1},{3,2},{4,3},{5,4},{6,5},{7,6},{8,7},{9,8},{10,9},{11,1... | collective-permute-start | bytes 49160 | tf_op jit(solution)/shard_map/ppermute | solution.py:596
  4.4 8.8 %collective-permute-start = (f32[16,8,128]{2,1,0:T(8,128)S(1)}, f32[16,8,128]{2,1,0:T(8,128)S(1)}, u32[]{:S(2)}, u32[]{:S(2)}) collective-permute-start(f32[16,8,128]{2,1,0:T(8,128)S(1)} %get-tuple-element.86), channel_id=1, source_target_pairs={{16,0},{17,1},{18,2},{19,3},{20,4},{21,5},{22,6},{23,7},{24,8},{25... | collective-permute-start | bytes 196616 | tf_op jit(solution)/shard_map/ppermute | solution.py:596
  13.2 0.7 convert_bitcast_fusion
  13.9 0.7 pad_maximum_fusion.donor_ref
  15.3 1.8 %shard_map.79 = (f32[16,24,128]{2,1,0:T(8,128)S(1)}, f32[32,1,1152]{2,1,0:T(1,128)}) custom-call(s32[3]{0:T(128)S(1)} %pad_add_fusion.2.place_ref, f32[16,16,128]{2,1,0:T(8,128)S(1)} %get-tuple-element.85.held_ref, f32[16,8,128]{2,1,0:T(8,128)S(1)} %collective-permute-done.south_ref, f32[2,16,128]{2,1,0:T(8,128)S(1)} %collective-permute-done.1.east_ref, ...), custom_call_target="tpu_custom_call" | custom-call | tf_op jit(solution)/shard_map/pallas_call | solution.py:609
  17.1 7.9 %all-to-all-start.3 = ((f32[32,1,1152]{2,1,0:T(1,128)}), f32[32,1,1152]{2,1,0:T(1,128)S(1)}, u32[]{:S(2)}, u32[]{:S(2)}) async-start(f32[32,1,1152]{2,1,0:T(1,128)} %get-tuple-element.93), calls=%async_computation.3 | async-start | bytes 294912 | tf_op jit(solution)/shard_map/all_to_all | solution.py:659
  24.9 0.8 slice_reduce_fusion.1
  25.7 0.8 slice_reduce_fusion
  27.0 3.1 %collective-permute-start.3 = (f32[2,24,128]{2,1,0:T(8,128)S(1)}, f32[2,24,128]{2,1,0:T(8,128)S(1)}, u32[]{:S(2)}, u32[]{:S(2)}) collective-permute-start(f32[2,24,128]{2,1,0:T(8,128)S(1)} %shard_map.81), channel_id=1, source_target_pairs={{0,1},{1,2},{2,3},{3,4},{4,5},{5,6},{6,7},{7,8},{8,9},{9,10},{10,1... | collective-permute-start | bytes 73736 | tf_op jit(solution)/shard_map/ppermute | solution.py:596
  31.0 1.8 %shard_map.80.send_ref = bf16[640,1024]{1,0:T(8,128)(2,1)S(1)} custom-call(s32[3]{0:T(128)S(1)} %pad_add_fusion.2.place_ref, s32[16,384]{1,0:T(8,128)S(1)} %get-tuple-element.100.holder_ref, s32[16,384]{1,0:T(8,128)S(1)} %get-tuple-element.119.spot_ref), custom_call_target="tpu_custom_call" | custom-call | tf_op jit(solution)/shard_map/pallas_call | solution.py:609
  32.8 1.6 %all-to-all-done.3.got_ref = f32[32,1,1152]{2,1,0:T(1,128)S(1)} async-done(((f32[32,1,1152]{2,1,0:T(1,128)}), f32[32,1,1152]{2,1,0:T(1,128)S(1)}, u32[]{:S(2)}, u32[]{:S(2)}) %all-to-all-start.3) | async-done | bytes 147488 | tf_op jit(solution)/shard_map/all_to_all | solution.py:659
  34.3 1.7 %shard_map.82 = (f32[16,16,128]{2,1,0:T(8,128)}, f32[16,8,128]{2,1,0:T(8,128)S(1)}) custom-call(s32[3]{0:T(128)S(1)} %pad_add_fusion.2.place_ref, f32[32,1,1152]{2,1,0:T(1,128)S(1)} %all-to-all-done.3.got_ref, bf16[640,1024]{1,0:T(8,128)(2,1)S(1)} %shard_map.80.send_ref, f32[16,24,128]{2,1,0:T(8,128)S(1)} %get-tuple-element.97.lower_ref, ...), custom_call_target="tpu_custom_call" | custom-call | tf_op jit(solution)/shard_map/pallas_call | solution.py:609
  36.0 10.7 %all-to-all-start.4 = ((f32[16,16,128]{2,1,0:T(8,128)}), f32[16,16,128]{2,1,0:T(8,128)S(1)}, u32[]{:S(2)}, u32[]{:S(2)}) async-start(f32[16,16,128]{2,1,0:T(8,128)} %get-tuple-element.99), calls=%async_computation.4 | async-start | bytes 262144 | tf_op jit(solution)/shard_map/all_to_all | solution.py:720
  46.7 3.5 %collective-permute-start.4 = (f32[16,8,128]{2,1,0:T(8,128)S(1)}, f32[16,8,128]{2,1,0:T(8,128)S(1)}, u32[]{:S(2)}, u32[]{:S(2)}) collective-permute-start(f32[16,8,128]{2,1,0:T(8,128)S(1)} %get-tuple-element.98), channel_id=1, source_target_pairs={{0,16},{1,17},{2,18},{3,19},{4,20},{5,21},{6,22},{7,23},{8,24},{9,... | collective-permute-start | bytes 196616 | tf_op jit(solution)/shard_map/ppermute | solution.py:596
  50.3 1.0 %shard_map.83 = (bf16[1024,384]{1,0:T(8,128)(2,1)S(1)}, f32[5,32,128]{2,1,0:T(8,128)S(1)}) custom-call(s32[3]{0:T(128)S(1)} %pad_add_fusion.2.place_ref, s32[16,384]{1,0:T(8,128)S(1)} %get-tuple-element.100.holder_ref), custom_call_target="tpu_custom_call" | custom-call | tf_op jit(solution)/shard_map/pallas_call | solution.py:609
  52.0 4.0 %all-to-all-done.4.got_ref = f32[16,16,128]{2,1,0:T(8,128)S(1)} async-done(((f32[16,16,128]{2,1,0:T(8,128)}), f32[16,16,128]{2,1,0:T(8,128)S(1)}, u32[]{:S(2)}, u32[]{:S(2)}) %all-to-all-start.4) | async-done | bytes 131104 | tf_op jit(solution)/shard_map/all_to_all | solution.py:720
  56.0 2.2 %shard_map.85 = (f32[16,24,128]{2,1,0:T(8,128)S(1)}, f32[32,1,1152]{2,1,0:T(1,128)S(1)}) custom-call(s32[3]{0:T(128)S(1)} %pad_add_fusion.2.place_ref, f32[2]{0:T(128)S(1)} %copy-done.1, f32[16,24,128]{2,1,0:T(8,128)S(1)} %get-tuple-element.97.lower_ref, f32[16,8,128]{2,1,0:T(8,128)S(1)} %collective-permute-done.4.north_ref, ...), custom_call_target="tpu_custom_call" | custom-call | tf_op jit(solution)/shard_map/pallas_call | solution.py:609
  58.2 16.5 %all_to_all.35.got_ref = f32[32,1,1152]{2,1,0:T(1,128)S(1)} all-to-all(f32[32,1,1152]{2,1,0:T(1,128)S(1)} %get-tuple-element.105), channel_id=1, replica_groups=mesh['panel'=2,'lat'=16,'lon'=16] {'panel','lon'}, dimensions={0} | all-to-all | bytes 294912 | tf_op jit(solution)/shard_map/all_to_all | solution.py:659
  74.7 1.7 %shard_map.86 = f32[16,16,128]{2,1,0:T(8,128)} custom-call(s32[3]{0:T(128)S(1)} %pad_add_fusion.2.place_ref, f32[32,1,1152]{2,1,0:T(1,128)S(1)} %all_to_all.35.got_ref, bf16[640,1024]{1,0:T(8,128)(2,1)S(1)} %shard_map.80.send_ref), custom_call_target="tpu_custom_call" | custom-call | tf_op jit(solution)/shard_map/pallas_call | solution.py:609
  76.4 6.0 %all-to-all-start.6 = ((f32[16,16,128]{2,1,0:T(8,128)}), f32[16,16,128]{2,1,0:T(8,128)S(1)}, u32[]{:S(2)}, u32[]{:S(2)}) async-start(f32[16,16,128]{2,1,0:T(8,128)} %shard_map.86), calls=%async_computation.6 | async-start | bytes 262144 | tf_op jit(solution)/shard_map/all_to_all | solution.py:720
  84.3 7.3 %all-to-all-done.6.got_ref = f32[16,16,128]{2,1,0:T(8,128)S(1)} async-done(((f32[16,16,128]{2,1,0:T(8,128)}), f32[16,16,128]{2,1,0:T(8,128)S(1)}, u32[]{:S(2)}, u32[]{:S(2)}) %all-to-all-start.6) | async-done | bytes 131104 | tf_op jit(solution)/shard_map/all_to_all | solution.py:720
  91.6 2.7 %shard_map.87 = (f32[8,4,16,48]{3,2,1,0:T(8,128)}, f32[8,4,16,48]{3,2,1,0:T(8,128)}) custom-call(s32[3]{0:T(128)S(1)} %pad_add_fusion.2.place_ref, f32[2]{0:T(128)S(1)} %copy-done.1, f32[16,24,128]{2,1,0:T(8,128)S(1)} %get-tuple-element.106.middle_ref, f32[16,16,128]{2,1,0:T(8,128)S(1)} %all-to-all-done.6.got_ref, ...), custom_call_target="tpu_custom_call" | custom-call | tf_op jit(solution)/shard_map/pallas_call | solution.py:609
  (32 shorter events, 3.5 us)
Async XLA Ops:
  0.6 1.0 %copy-start = (f32[1,8,4,16,48]{4,3,2,1,0:T(8,128)S(1)}, f32[1,8,4,16,48]{4,3,2,1,0:T(8,128)}, u32[]{:S(2)}) copy-start(f32[1,8,4,16,48]{4,3,2,1,0:T(8,128)} %param.8) | copy-start | bytes 294916
  1.8 13.0 %collective-permute-start.2 = (f32[2,8,128]{2,1,0:T(8,128)S(1)}, f32[2,8,128]{2,1,0:T(8,128)S(1)}, u32[]{:S(2)}, u32[]{:S(2)}) collective-permute-start(f32[2,8,128]{2,1,0:T(8,128)S(1)} %get-tuple-element.88), channel_id=1, source_target_pairs={{17,0},{18,1},{19,2},{20,3},{21,4},{22,5},{23,6},{24,7},{25,8},{26... | collective-permute-start | bytes 24584 | tf_op jit(solution)/shard_map/ppermute | solution.py:596
  3.1 12.2 %collective-permute-start.1 = (f32[2,16,128]{2,1,0:T(8,128)S(1)}, f32[2,16,128]{2,1,0:T(8,128)S(1)}, u32[]{:S(2)}, u32[]{:S(2)}) collective-permute-start(f32[2,16,128]{2,1,0:T(8,128)S(1)} %get-tuple-element.87), channel_id=1, source_target_pairs={{1,0},{2,1},{3,2},{4,3},{5,4},{6,5},{7,6},{8,7},{9,8},{10,9},{11,1... | collective-permute-start | bytes 49160 | tf_op jit(solution)/shard_map/ppermute | solution.py:596
  4.4 10.9 %collective-permute-start = (f32[16,8,128]{2,1,0:T(8,128)S(1)}, f32[16,8,128]{2,1,0:T(8,128)S(1)}, u32[]{:S(2)}, u32[]{:S(2)}) collective-permute-start(f32[16,8,128]{2,1,0:T(8,128)S(1)} %get-tuple-element.86), channel_id=1, source_target_pairs={{16,0},{17,1},{18,2},{19,3},{20,4},{21,5},{22,6},{23,7},{24,8},{25... | collective-permute-start | bytes 196616 | tf_op jit(solution)/shard_map/ppermute | solution.py:596
  17.1 17.3 %all-to-all-start.3 = ((f32[32,1,1152]{2,1,0:T(1,128)}), f32[32,1,1152]{2,1,0:T(1,128)S(1)}, u32[]{:S(2)}, u32[]{:S(2)}) async-start(f32[32,1,1152]{2,1,0:T(1,128)} %get-tuple-element.93), calls=%async_computation.3 | async-start | bytes 294912 | tf_op jit(solution)/shard_map/all_to_all | solution.py:659
  27.0 5.7 %collective-permute-start.3 = (f32[2,24,128]{2,1,0:T(8,128)S(1)}, f32[2,24,128]{2,1,0:T(8,128)S(1)}, u32[]{:S(2)}, u32[]{:S(2)}) collective-permute-start(f32[2,24,128]{2,1,0:T(8,128)S(1)} %shard_map.81), channel_id=1, source_target_pairs={{0,1},{1,2},{2,3},{3,4},{4,5},{5,6},{6,7},{7,8},{8,9},{9,10},{10,1... | collective-permute-start | bytes 73736 | tf_op jit(solution)/shard_map/ppermute | solution.py:596
  32.7 23.2 %copy-start.1 = (f32[2]{0:T(128)S(1)}, f32[2]{0:T(128)}, u32[]{:S(2)}) copy-start(f32[2]{0:T(128)} %diffusion_ref.3) | copy-start | bytes 28
  36.0 19.9 %all-to-all-start.4 = ((f32[16,16,128]{2,1,0:T(8,128)}), f32[16,16,128]{2,1,0:T(8,128)S(1)}, u32[]{:S(2)}, u32[]{:S(2)}) async-start(f32[16,16,128]{2,1,0:T(8,128)} %get-tuple-element.99), calls=%async_computation.4 | async-start | bytes 262144 | tf_op jit(solution)/shard_map/all_to_all | solution.py:720
  46.7 5.3 %collective-permute-start.4 = (f32[16,8,128]{2,1,0:T(8,128)S(1)}, f32[16,8,128]{2,1,0:T(8,128)S(1)}, u32[]{:S(2)}, u32[]{:S(2)}) collective-permute-start(f32[16,8,128]{2,1,0:T(8,128)S(1)} %get-tuple-element.98), channel_id=1, source_target_pairs={{0,16},{1,17},{2,18},{3,19},{4,20},{5,21},{6,22},{7,23},{8,24},{9,... | collective-permute-start | bytes 196616 | tf_op jit(solution)/shard_map/ppermute | solution.py:596
  76.4 15.2 %all-to-all-start.6 = ((f32[16,16,128]{2,1,0:T(8,128)}), f32[16,16,128]{2,1,0:T(8,128)S(1)}, u32[]{:S(2)}, u32[]{:S(2)}) async-start(f32[16,16,128]{2,1,0:T(8,128)} %shard_map.86), calls=%async_computation.6 | async-start | bytes 262144 | tf_op jit(solution)/shard_map/all_to_all | solution.py:720

commit v2 on v1

--- a/solution.py
+++ b/solution.py
@@ -189,7 +189,7 @@
 
 def donor_kernel(
     place_ref, held_ref, south_ref, east_ref, corner_ref, pick_ref, mix_ref, spin_ref,
-    lower_ref, out_ref
+    lower_ref, north_ref, out_ref
 ):
     column = column_of((ROWS, WIDE))
     beyond = column >= 8 + COLS
@@ -199,19 +199,10 @@
         corner = turn(corner_ref[group], 8 + COLS - 8 * which)
         lower_ref[pair, :ROWS] = jnp.where(beyond, east, held_ref[pair])
         lower_ref[pair, ROWS:] = jnp.where(beyond[:8], corner, south_ref[pair])
+        north_ref[pair] = lower_ref[pair, 8:16]
     planes = lower_ref[...].reshape(PAIRS * MID, WIDE)
     packed = donor_message(planes, pick_ref[...], mix_ref[...], spin_ref[...])
     post_message(place_ref, packed, jnp.zeros((1, WIDE), jnp.float32), out_ref)
-
-
-def last_kernel(lower_ref, west_ref):
-    column = column_of((MID, WIDE))
-    for group in range(2):
-        columns = jnp.zeros((MID, WIDE), jnp.float32)
-        for which in range(8):
-            moved = turn(lower_ref[8 * group + which], 8 * which - COLS)
-            columns = jnp.where(column // 8 == which, moved, columns)
-        west_ref[group] = columns
 
 
 def split_parts(held):
@@ -296,12 +287,16 @@
     coef_ref[4] = twirl * jnp.where(yang, jnp.cos(longitude), 0.0)
 
 
-def widen_kernel(place_ref, got_ref, send_ref, lower_ref, west_ref, out_ref, edge_ref):
-    column = column_of((8, WIDE))
-    for pair in range(PAIRS):
-        group, which = pair // 8, pair % 8
-        west = turn(west_ref[group, 8:16], -8 * which)
-        edge_ref[pair] = jnp.where(column < 8, west, lower_ref[pair, 8:16])
+def widen_kernel(place_ref, got_ref, send_ref, lower_ref, north_ref, out_ref, west_ref):
+    column = column_of((TALL, WIDE))
+    for group in range(2):
+        columns = jnp.zeros((TALL, WIDE), jnp.float32)
+        for which in range(8):
+            pair = 8 * group + which
+            rows = jnp.concatenate([north_ref[pair], lower_ref[pair]], axis=0)
+            moved = turn(rows, 8 * which - COLS)
+            columns = jnp.where(column // 8 == which, moved, columns)
+        west_ref[group] = columns
     choice_kernel(place_ref, got_ref, send_ref, out_ref)
 
 
@@ -525,8 +520,8 @@
     for pair in range(PAIRS):
         group, which = pair // 8, pair % 8
         west = turn(west_ref[group], -8 * which)
-        work_ref[pair, :8] = north_ref[pair]
-        work_ref[pair, 8:] = jnp.where(column[8:] < 8, west, lower_ref[pair])
+        rows = jnp.concatenate([north_ref[pair], lower_ref[pair]], axis=0)
+        work_ref[pair] = jnp.where(column < 8, west, rows)
     ghosts = ghost_values(got_ref, take_ref)
     fill_ghosts(place_ref, ghosts, work_ref, TALL)
 
@@ -641,9 +636,9 @@
         scratch=[pltpu.VMEM((1, WIDE), f32)],
     )
     message = ((2 * PEERS, 1, MESSAGE), f32)
-    lower, sent = call(
+    lower, north, sent = call(
         donor_kernel,
-        [((PAIRS, MID, WIDE), f32), message],
+        [((PAIRS, MID, WIDE), f32), ((PAIRS, 8, WIDE), f32), message],
         place,
         held,
         south,
@@ -660,12 +655,10 @@
 
     got = to_holders(sent)
 
-    late_lat, late_lon, border, late_lower, _ = lax.optimization_barrier(
-        (lat, lon, border_source, lower, sent)
-    )
-    border = border[0]
-    (west,) = call(last_kernel, [((2, MID, WIDE), f32)], late_lower)
-    west = shift(west, 0, 1)
+    north, late_lat, late_lon, border, _ = lax.optimization_barrier(
+        (north, lat, lon, border_source[0], sent)
+    )
+    north = shift(north, 1, 0)
 
     ring = PANEL_COLS + 8
     row_slots = LONS * SLOTS
@@ -696,10 +689,10 @@
     )
     chunk = ((PEERS, 16, WIDE), f32)
     first_got = got
-    chunks, north = call(
-        widen_kernel, [chunk, ((PAIRS, 8, WIDE), f32)], place, got, send, lower, west, smem=1
-    )
-    north = shift(north, 1, 0)
+    chunks, west = call(
+        widen_kernel, [chunk, ((2, TALL, WIDE), f32)], place, got, send, lower, north, smem=1
+    )
+    west = shift(west, 0, 1)
     late_holder, bands, sides, _ = lax.optimization_barrier((holder, bands, sides, chunks))
     take, coef = call(
         take_kernel,

time: 94.9 us -> 93.3 us (0.983)
  blocking collectives: 16.5 us -> 13.8 us
  local copies, waits for them, and re-layouts: 4.07 us -> 2.62 us
  waiting for transfers between devices: 13.5 us -> 14.8 us
    all_to_all x1, blocking collectives: 16.5 us -> 13.8 us  [to_holders(): return lax.all_to_all(sent, ('panel', 'lon'), 0, 0, tiled=True)]
    all_to_all x1, waiting for transfers between devices: 1.57 us -> 3.59 us  [to_holders(): return lax.all_to_all(sent, ('panel', 'lon'), 0, 0, tiled=True)]
    all_to_all x2, starting transfers between devices: 16.7 us -> 17.9 us  [to_blocks(): return lax.all_to_all(chunks, 'lat', 0, 0, tiled=True)]
    pallas_call x11 -> x10, Pallas kernels: 13.7 us -> 13.6 us  [call(): pl.pallas_call(kernel, out_shape=shapes, in_specs=specs or [SMEM] * smem...]
  transfers between devices with their start and end apart: 8 -> 8, of which waited for: 5 -> 3; matrix products, arithmetic and copies ran while one was open for 5% -> 4% of each run, Pallas kernels for 4% -> 4%
where the time goes in v2:
time: 93.3 us; the launch traced here: 92.7 us
  starting transfers between devices  43.2 us (46%)
  waiting for transfers between devices  14.8 us (16%)
  blocking collectives  13.8 us (15%)
  Pallas kernels  13.6 us (15%)
  local copies, waits for them, and re-layouts  2.62 us (3%)
  other arithmetic  2.55 us (3%)
  between operations  2.21 us (2%)
    all_to_all x2, starting transfers between devices, to_blocks(): return lax.all_to_all(chunks, 'lat', 0, 0, tiled=True)  17.9 us
    ppermute x5, starting transfers between devices, shift(): return lax.ppermute(value, ('lat', 'lon'), pairs)  17.7 us
    all_to_all x1, blocking collectives, to_holders(): return lax.all_to_all(sent, ('panel', 'lon'), 0, 0, tiled=True)  13.8 us
    pallas_call x10, Pallas kernels, call(): pl.pallas_call(kernel, out_shape=shapes, in_specs=specs or [SMEM] * smem...  13.6 us
    all_to_all x2, waiting for transfers between devices, to_blocks(): return lax.all_to_all(chunks, 'lat', 0, 0, tiled=True)  11.2 us
    all_to_all x1, starting transfers between devices, to_holders(): return lax.all_to_all(sent, ('panel', 'lon'), 0, 0, tiled=True)  7.51 us
    all_to_all x1, waiting for transfers between devices, to_holders(): return lax.all_to_all(sent, ('panel', 'lon'), 0, 0, tiled=True)  3.59 us
  transfers between devices with their start and end apart: 8, of which 3 were waited for; matrix products, arithmetic and copies ran while one was open for 4% of the time, Pallas kernels for 4%

profile of v2, /device:TPU:1, one launch (start us, length us, event | category | flops | bytes accessed | tf_op | source)
XLA Modules:
  0.0 92.7 jit_solution(16197101941913356789)
XLA Ops:
  0.6 0.9 %copy-done = f32[1,8,4,16,48]{4,3,2,1,0:T(8,128)S(1)} copy-done((f32[1,8,4,16,48]{4,3,2,1,0:T(8,128)S(1)}, f32[1,8,4,16,48]{4,3,2,1,0:T(8,128)}, u32[]{:S(2)}) %copy-start) | copy-done | bytes 98328
  1.8 1.3 %collective-permute-start.2 = (f32[2,8,128]{2,1,0:T(8,128)S(1)}, f32[2,8,128]{2,1,0:T(8,128)S(1)}, u32[]{:S(2)}, u32[]{:S(2)}) collective-permute-start(f32[2,8,128]{2,1,0:T(8,128)S(1)} %get-tuple-element.89), channel_id=1, source_target_pairs={{17,0},{18,1},{19,2},{20,3},{21,4},{22,5},{23,6},{24,7},{25,8},{26... | collective-permute-start | bytes 24584 | tf_op jit(solution)/shard_map/ppermute | solution.py:591
  3.1 1.3 %collective-permute-start.1 = (f32[2,16,128]{2,1,0:T(8,128)S(1)}, f32[2,16,128]{2,1,0:T(8,128)S(1)}, u32[]{:S(2)}, u32[]{:S(2)}) collective-permute-start(f32[2,16,128]{2,1,0:T(8,128)S(1)} %get-tuple-element.88), channel_id=1, source_target_pairs={{1,0},{2,1},{3,2},{4,3},{5,4},{6,5},{7,6},{8,7},{9,8},{10,9},{11,1... | collective-permute-start | bytes 49160 | tf_op jit(solution)/shard_map/ppermute | solution.py:591
  4.4 8.8 %collective-permute-start = (f32[16,8,128]{2,1,0:T(8,128)S(1)}, f32[16,8,128]{2,1,0:T(8,128)S(1)}, u32[]{:S(2)}, u32[]{:S(2)}) collective-permute-start(f32[16,8,128]{2,1,0:T(8,128)S(1)} %get-tuple-element.87), channel_id=1, source_target_pairs={{16,0},{17,1},{18,2},{19,3},{20,4},{21,5},{22,6},{23,7},{24,8},{25... | collective-permute-start | bytes 196616 | tf_op jit(solution)/shard_map/ppermute | solution.py:591
  13.2 0.7 convert_bitcast_fusion
  13.9 0.7 pad_maximum_fusion.donor_ref
  14.8 0.8 reduce
  15.7 1.8 %shard_map.79 = (f32[16,24,128]{2,1,0:T(8,128)S(1)}, f32[16,8,128]{2,1,0:T(8,128)S(1)}, f32[32,1,1152]{2,1,0:T(1,128)}) custom-call(s32[3]{0:T(128)S(1)} %pad_add_fusion.2.place_ref, f32[16,16,128]{2,1,0:T(8,128)S(1)} %get-tuple-element.86.held_ref, f32[16,8,128]{2,1,0:T(8,128)S(1)} %collective-permute-done.south_ref, ...), custom_call_target="tpu_custom_call" | custom-call | tf_op jit(solution)/shard_map/pallas_call | solution.py:604
  17.5 7.5 %all-to-all-start.3 = ((f32[32,1,1152]{2,1,0:T(1,128)}), f32[32,1,1152]{2,1,0:T(1,128)S(1)}, u32[]{:S(2)}, u32[]{:S(2)}) async-start(f32[32,1,1152]{2,1,0:T(1,128)} %get-tuple-element.95), calls=%async_computation.3 | async-start | bytes 294912 | tf_op jit(solution)/shard_map/all_to_all | solution.py:654
  25.4 2.8 %collective-permute-start.3 = (f32[16,8,128]{2,1,0:T(8,128)S(1)}, f32[16,8,128]{2,1,0:T(8,128)S(1)}, u32[]{:S(2)}, u32[]{:S(2)}) collective-permute-start(f32[16,8,128]{2,1,0:T(8,128)S(1)} %get-tuple-element.96), channel_id=1, source_target_pairs={{0,16},{1,17},{2,18},{3,19},{4,20},{5,21},{6,22},{7,23},{8,24},{9,... | collective-permute-start | bytes 196616 | tf_op jit(solution)/shard_map/ppermute | solution.py:591
  29.0 1.8 %shard_map.80.send_ref = bf16[640,1024]{1,0:T(8,128)(2,1)S(1)} custom-call(s32[3]{0:T(128)S(1)} %pad_add_fusion.2.place_ref, s32[16,384]{1,0:T(8,128)S(1)} %get-tuple-element.102.holder_ref, s32[16,384]{1,0:T(8,128)S(1)} %get-tuple-element.121.spot_ref), custom_call_target="tpu_custom_call" | custom-call | tf_op jit(solution)/shard_map/pallas_call | solution.py:604
  30.8 3.6 %all-to-all-done.3.got_ref = f32[32,1,1152]{2,1,0:T(1,128)S(1)} async-done(((f32[32,1,1152]{2,1,0:T(1,128)}), f32[32,1,1152]{2,1,0:T(1,128)S(1)}, u32[]{:S(2)}, u32[]{:S(2)}) %all-to-all-start.3) | async-done | bytes 147488 | tf_op jit(solution)/shard_map/all_to_all | solution.py:654
  34.4 1.7 %shard_map.81 = (f32[16,16,128]{2,1,0:T(8,128)}, f32[2,32,128]{2,1,0:T(8,128)S(1)}) custom-call(s32[3]{0:T(128)S(1)} %pad_add_fusion.2.place_ref, f32[32,1,1152]{2,1,0:T(1,128)S(1)} %all-to-all-done.3.got_ref, bf16[640,1024]{1,0:T(8,128)(2,1)S(1)} %shard_map.80.send_ref, f32[16,24,128]{2,1,0:T(8,128)S(1)} %get-tuple-element.93.lower_ref, ...), custom_call_target="tpu_custom_call" | custom-call | tf_op jit(solution)/shard_map/pallas_call | solution.py:604
  36.1 11.5 %all-to-all-start.4 = ((f32[16,16,128]{2,1,0:T(8,128)}), f32[16,16,128]{2,1,0:T(8,128)S(1)}, u32[]{:S(2)}, u32[]{:S(2)}) async-start(f32[16,16,128]{2,1,0:T(8,128)} %get-tuple-element.101), calls=%async_computation.4 | async-start | bytes 262144 | tf_op jit(solution)/shard_map/all_to_all | solution.py:713
  47.5 3.6 %collective-permute-start.4 = (f32[2,32,128]{2,1,0:T(8,128)S(1)}, f32[2,32,128]{2,1,0:T(8,128)S(1)}, u32[]{:S(2)}, u32[]{:S(2)}) collective-permute-start(f32[2,32,128]{2,1,0:T(8,128)S(1)} %get-tuple-element.100), channel_id=1, source_target_pairs={{0,1},{1,2},{2,3},{3,4},{4,5},{5,6},{6,7},{7,8},{8,9},{9,10},{10,1... | collective-permute-start | bytes 98312 | tf_op jit(solution)/shard_map/ppermute | solution.py:591
  51.2 1.0 %shard_map.82 = (bf16[1024,384]{1,0:T(8,128)(2,1)S(1)}, f32[5,32,128]{2,1,0:T(8,128)S(1)}) custom-call(s32[3]{0:T(128)S(1)} %pad_add_fusion.2.place_ref, s32[16,384]{1,0:T(8,128)S(1)} %get-tuple-element.102.holder_ref), custom_call_target="tpu_custom_call" | custom-call | tf_op jit(solution)/shard_map/pallas_call | solution.py:604
  52.7 4.0 %all-to-all-done.4.got_ref = f32[16,16,128]{2,1,0:T(8,128)S(1)} async-done(((f32[16,16,128]{2,1,0:T(8,128)}), f32[16,16,128]{2,1,0:T(8,128)S(1)}, u32[]{:S(2)}, u32[]{:S(2)}) %all-to-all-start.4) | async-done | bytes 131104 | tf_op jit(solution)/shard_map/all_to_all | solution.py:713
  56.7 2.2 %shard_map.84 = (f32[16,24,128]{2,1,0:T(8,128)S(1)}, f32[32,1,1152]{2,1,0:T(1,128)S(1)}) custom-call(s32[3]{0:T(128)S(1)} %pad_add_fusion.2.place_ref, f32[2]{0:T(128)S(1)} %copy-done.1, f32[16,24,128]{2,1,0:T(8,128)S(1)} %get-tuple-element.93.lower_ref, f32[16,8,128]{2,1,0:T(8,128)S(1)} %collective-permute-done.3.north_ref, ...), custom_call_target="tpu_custom_call" | custom-call | tf_op jit(solution)/shard_map/pallas_call | solution.py:604
  58.9 13.8 %all_to_all.35.got_ref = f32[32,1,1152]{2,1,0:T(1,128)S(1)} all-to-all(f32[32,1,1152]{2,1,0:T(1,128)S(1)} %get-tuple-element.107), channel_id=1, replica_groups=mesh['panel'=2,'lat'=16,'lon'=16] {'panel','lon'}, dimensions={0} | all-to-all | bytes 294912 | tf_op jit(solution)/shard_map/all_to_all | solution.py:654
  72.7 1.7 %shard_map.85 = f32[16,16,128]{2,1,0:T(8,128)} custom-call(s32[3]{0:T(128)S(1)} %pad_add_fusion.2.place_ref, f32[32,1,1152]{2,1,0:T(1,128)S(1)} %all_to_all.35.got_ref, bf16[640,1024]{1,0:T(8,128)(2,1)S(1)} %shard_map.80.send_ref), custom_call_target="tpu_custom_call" | custom-call | tf_op jit(solution)/shard_map/pallas_call | solution.py:604
  74.4 6.5 %all-to-all-start.6 = ((f32[16,16,128]{2,1,0:T(8,128)}), f32[16,16,128]{2,1,0:T(8,128)S(1)}, u32[]{:S(2)}, u32[]{:S(2)}) async-start(f32[16,16,128]{2,1,0:T(8,128)} %shard_map.85), calls=%async_computation.6 | async-start | bytes 262144 | tf_op jit(solution)/shard_map/all_to_all | solution.py:713
  80.9 0.7 fusion.4
  82.9 7.2 %all-to-all-done.6.got_ref = f32[16,16,128]{2,1,0:T(8,128)S(1)} async-done(((f32[16,16,128]{2,1,0:T(8,128)}), f32[16,16,128]{2,1,0:T(8,128)S(1)}, u32[]{:S(2)}, u32[]{:S(2)}) %all-to-all-start.6) | async-done | bytes 131104 | tf_op jit(solution)/shard_map/all_to_all | solution.py:713
  90.0 2.7 %shard_map.86 = (f32[8,4,16,48]{3,2,1,0:T(8,128)}, f32[8,4,16,48]{3,2,1,0:T(8,128)}) custom-call(s32[3]{0:T(128)S(1)} %pad_add_fusion.2.place_ref, f32[2]{0:T(128)S(1)} %copy-done.1, f32[16,24,128]{2,1,0:T(8,128)S(1)} %get-tuple-element.108.middle_ref, f32[16,16,128]{2,1,0:T(8,128)S(1)} %all-to-all-done.6.got_ref, ...), custom_call_target="tpu_custom_call" | custom-call | tf_op jit(solution)/shard_map/pallas_call | solution.py:604
  (32 shorter events, 2.2 us)
Async XLA Ops:
  0.6 1.0 %copy-start = (f32[1,8,4,16,48]{4,3,2,1,0:T(8,128)S(1)}, f32[1,8,4,16,48]{4,3,2,1,0:T(8,128)}, u32[]{:S(2)}) copy-start(f32[1,8,4,16,48]{4,3,2,1,0:T(8,128)} %param.8) | copy-start | bytes 294916
  1.8 13.9 %collective-permute-start.2 = (f32[2,8,128]{2,1,0:T(8,128)S(1)}, f32[2,8,128]{2,1,0:T(8,128)S(1)}, u32[]{:S(2)}, u32[]{:S(2)}) collective-permute-start(f32[2,8,128]{2,1,0:T(8,128)S(1)} %get-tuple-element.89), channel_id=1, source_target_pairs={{17,0},{18,1},{19,2},{20,3},{21,4},{22,5},{23,6},{24,7},{25,8},{26... | collective-permute-start | bytes 24584 | tf_op jit(solution)/shard_map/ppermute | solution.py:591
  3.1 12.6 %collective-permute-start.1 = (f32[2,16,128]{2,1,0:T(8,128)S(1)}, f32[2,16,128]{2,1,0:T(8,128)S(1)}, u32[]{:S(2)}, u32[]{:S(2)}) collective-permute-start(f32[2,16,128]{2,1,0:T(8,128)S(1)} %get-tuple-element.88), channel_id=1, source_target_pairs={{1,0},{2,1},{3,2},{4,3},{5,4},{6,5},{7,6},{8,7},{9,8},{10,9},{11,1... | collective-permute-start | bytes 49160 | tf_op jit(solution)/shard_map/ppermute | solution.py:591
  4.4 11.3 %collective-permute-start = (f32[16,8,128]{2,1,0:T(8,128)S(1)}, f32[16,8,128]{2,1,0:T(8,128)S(1)}, u32[]{:S(2)}, u32[]{:S(2)}) collective-permute-start(f32[16,8,128]{2,1,0:T(8,128)S(1)} %get-tuple-element.87), channel_id=1, source_target_pairs={{16,0},{17,1},{18,2},{19,3},{20,4},{21,5},{22,6},{23,7},{24,8},{25... | collective-permute-start | bytes 196616 | tf_op jit(solution)/shard_map/ppermute | solution.py:591
  17.5 16.9 %all-to-all-start.3 = ((f32[32,1,1152]{2,1,0:T(1,128)}), f32[32,1,1152]{2,1,0:T(1,128)S(1)}, u32[]{:S(2)}, u32[]{:S(2)}) async-start(f32[32,1,1152]{2,1,0:T(1,128)} %get-tuple-element.95), calls=%async_computation.3 | async-start | bytes 294912 | tf_op jit(solution)/shard_map/all_to_all | solution.py:654
  25.4 5.4 %collective-permute-start.3 = (f32[16,8,128]{2,1,0:T(8,128)S(1)}, f32[16,8,128]{2,1,0:T(8,128)S(1)}, u32[]{:S(2)}, u32[]{:S(2)}) collective-permute-start(f32[16,8,128]{2,1,0:T(8,128)S(1)} %get-tuple-element.96), channel_id=1, source_target_pairs={{0,16},{1,17},{2,18},{3,19},{4,20},{5,21},{6,22},{7,23},{8,24},{9,... | collective-permute-start | bytes 196616 | tf_op jit(solution)/shard_map/ppermute | solution.py:591
  30.7 25.9 %copy-start.1 = (f32[2]{0:T(128)S(1)}, f32[2]{0:T(128)}, u32[]{:S(2)}) copy-start(f32[2]{0:T(128)} %diffusion_ref.3) | copy-start | bytes 28
  36.1 20.6 %all-to-all-start.4 = ((f32[16,16,128]{2,1,0:T(8,128)}), f32[16,16,128]{2,1,0:T(8,128)S(1)}, u32[]{:S(2)}, u32[]{:S(2)}) async-start(f32[16,16,128]{2,1,0:T(8,128)} %get-tuple-element.101), calls=%async_computation.4 | async-start | bytes 262144 | tf_op jit(solution)/shard_map/all_to_all | solution.py:713
  47.5 5.2 %collective-permute-start.4 = (f32[2,32,128]{2,1,0:T(8,128)S(1)}, f32[2,32,128]{2,1,0:T(8,128)S(1)}, u32[]{:S(2)}, u32[]{:S(2)}) collective-permute-start(f32[2,32,128]{2,1,0:T(8,128)S(1)} %get-tuple-element.100), channel_id=1, source_target_pairs={{0,1},{1,2},{2,3},{3,4},{4,5},{5,6},{6,7},{7,8},{8,9},{9,10},{10,1... | collective-permute-start | bytes 98312 | tf_op jit(solution)/shard_map/ppermute | solution.py:591
  74.4 15.6 %all-to-all-start.6 = ((f32[16,16,128]{2,1,0:T(8,128)}), f32[16,16,128]{2,1,0:T(8,128)S(1)}, u32[]{:S(2)}, u32[]{:S(2)}) async-start(f32[16,16,128]{2,1,0:T(8,128)} %shard_map.85), calls=%async_computation.6 | async-start | bytes 262144 | tf_op jit(solution)/shard_map/all_to_all | solution.py:713

commit v3 on v2

--- a/solution.py
+++ b/solution.py
@@ -375,15 +375,22 @@
             lines.append(jnp.where(low, one, pltpu.roll(two, HALF, 1)))
             lines.append(jnp.where(low, pltpu.roll(one, HALF, 1), two))
 
+        def put(first):
+            tile = first // 8 * 8
+            row = iota((8, WIDE), 0)
+            held = work_ref[:, tile : tile + 8, :]
+            for which in range(4):
+                mask = row == first - tile + which
+                held = jnp.where(mask[None], lines[which][:, None, :], held)
+            work_ref[:, tile : tile + 8, :] = held
+
         @pl.when(lat == 0)
         def _():
-            for row in range(4):
-                work_ref[:, top - 4 + row, :] = lines[row]
+            put(top - 4)
 
         @pl.when(lat == LATS - 1)
         def _():
-            for row in range(4):
-                work_ref[:, top + ROWS + row, :] = lines[row]
+            put(top + ROWS)
 
 
 def rates(load, rows, coef_ref, diffusion_ref):
@@ -656,8 +663,9 @@
     got = to_holders(sent)
 
     north, late_lat, late_lon, border, _ = lax.optimization_barrier(
-        (north, lat, lon, border_source[0], sent)
-    )
+        (north, lat, lon, border_source, sent)
+    )
+    border = lax.optimization_barrier(border[0])
     north = shift(north, 1, 0)
 
     ring = PANEL_COLS + 8

time: 93.3 us -> 93.6 us (level)
  starting transfers between devices: 43.2 us -> 41.9 us
  blocking collectives: 13.8 us -> 14.8 us
    all_to_all x1, blocking collectives: 13.8 us -> 14.8 us  [to_holders(): return lax.all_to_all(sent, ('panel', 'lon'), 0, 0, tiled=True)]
  transfers between devices with their start and end apart: 8 -> 8, of which waited for: 3 -> 4; matrix products, arithmetic and copies ran while one was open for 4% -> 5% of each run, Pallas kernels for 4% -> 4%
where the time goes in v3:
time: 93.6 us; the launch traced here: 92.9 us
  starting transfers between devices  41.9 us (45%)
  waiting for transfers between devices  15.2 us (16%)
  blocking collectives  14.8 us (16%)
  Pallas kernels  13.6 us (15%)
  local copies, waits for them, and re-layouts  2.62 us (3%)
  other arithmetic  2.55 us (3%)
  between operations  2.19 us (2%)
    all_to_all x2, starting transfers between devices, to_blocks(): return lax.all_to_all(chunks, 'lat', 0, 0, tiled=True)  17.2 us
    ppermute x5, starting transfers between devices, shift(): return lax.ppermute(value, ('lat', 'lon'), pairs)  16.9 us
    all_to_all x1, blocking collectives, to_holders(): return lax.all_to_all(sent, ('panel', 'lon'), 0, 0, tiled=True)  14.8 us
    pallas_call x10, Pallas kernels, call(): pl.pallas_call(kernel, out_shape=shapes, in_specs=specs or [SMEM] * smem...  13.6 us
    all_to_all x2, waiting for transfers between devices, to_blocks(): return lax.all_to_all(chunks, 'lat', 0, 0, tiled=True)  11.4 us
    all_to_all x1, starting transfers between devices, to_holders(): return lax.all_to_all(sent, ('panel', 'lon'), 0, 0, tiled=True)  7.87 us
    all_to_all x1, waiting for transfers between devices, to_holders(): return lax.all_to_all(sent, ('panel', 'lon'), 0, 0, tiled=True)  3.34 us
  transfers between devices with their start and end apart: 8, of which 4 were waited for; matrix products, arithmetic and copies ran while one was open for 5% of the time, Pallas kernels for 4%

profile of v3, /device:TPU:1, one launch (start us, length us, event | category | flops | bytes accessed | tf_op | source)
XLA Modules:
  0.0 92.9 jit_solution(7618489564706478320)
XLA Ops:
  0.6 0.9 %copy-done = f32[1,8,4,16,48]{4,3,2,1,0:T(8,128)S(1)} copy-done((f32[1,8,4,16,48]{4,3,2,1,0:T(8,128)S(1)}, f32[1,8,4,16,48]{4,3,2,1,0:T(8,128)}, u32[]{:S(2)}) %copy-start) | copy-done | bytes 98328
  1.8 1.3 %collective-permute-start.2 = (f32[2,8,128]{2,1,0:T(8,128)S(1)}, f32[2,8,128]{2,1,0:T(8,128)S(1)}, u32[]{:S(2)}, u32[]{:S(2)}) collective-permute-start(f32[2,8,128]{2,1,0:T(8,128)S(1)} %get-tuple-element.89), channel_id=1, source_target_pairs={{17,0},{18,1},{19,2},{20,3},{21,4},{22,5},{23,6},{24,7},{25,8},{26... | collective-permute-start | bytes 24584 | tf_op jit(solution)/shard_map/ppermute | solution.py:598
  3.1 1.3 %collective-permute-start.1 = (f32[2,16,128]{2,1,0:T(8,128)S(1)}, f32[2,16,128]{2,1,0:T(8,128)S(1)}, u32[]{:S(2)}, u32[]{:S(2)}) collective-permute-start(f32[2,16,128]{2,1,0:T(8,128)S(1)} %get-tuple-element.88), channel_id=1, source_target_pairs={{1,0},{2,1},{3,2},{4,3},{5,4},{6,5},{7,6},{8,7},{9,8},{10,9},{11,1... | collective-permute-start | bytes 49160 | tf_op jit(solution)/shard_map/ppermute | solution.py:598
  4.4 8.8 %collective-permute-start = (f32[16,8,128]{2,1,0:T(8,128)S(1)}, f32[16,8,128]{2,1,0:T(8,128)S(1)}, u32[]{:S(2)}, u32[]{:S(2)}) collective-permute-start(f32[16,8,128]{2,1,0:T(8,128)S(1)} %get-tuple-element.87), channel_id=1, source_target_pairs={{16,0},{17,1},{18,2},{19,3},{20,4},{21,5},{22,6},{23,7},{24,8},{25... | collective-permute-start | bytes 196616 | tf_op jit(solution)/shard_map/ppermute | solution.py:598
  13.2 0.7 convert_bitcast_fusion
  13.9 0.7 pad_maximum_fusion.donor_ref
  15.3 1.8 %shard_map.79 = (f32[16,24,128]{2,1,0:T(8,128)S(1)}, f32[16,8,128]{2,1,0:T(8,128)S(1)}, f32[32,1,1152]{2,1,0:T(1,128)}) custom-call(s32[3]{0:T(128)S(1)} %pad_add_fusion.2.place_ref, f32[16,16,128]{2,1,0:T(8,128)S(1)} %get-tuple-element.86.held_ref, f32[16,8,128]{2,1,0:T(8,128)S(1)} %collective-permute-done.south_ref, ...), custom_call_target="tpu_custom_call" | custom-call | tf_op jit(solution)/shard_map/pallas_call | solution.py:611
  17.1 7.9 %all-to-all-start.3 = ((f32[32,1,1152]{2,1,0:T(1,128)}), f32[32,1,1152]{2,1,0:T(1,128)S(1)}, u32[]{:S(2)}, u32[]{:S(2)}) async-start(f32[32,1,1152]{2,1,0:T(1,128)} %get-tuple-element.95), calls=%async_computation.3 | async-start | bytes 294912 | tf_op jit(solution)/shard_map/all_to_all | solution.py:661
  24.9 0.8 reduce
  26.2 2.1 %collective-permute-start.3 = (f32[16,8,128]{2,1,0:T(8,128)S(1)}, f32[16,8,128]{2,1,0:T(8,128)S(1)}, u32[]{:S(2)}, u32[]{:S(2)}) collective-permute-start(f32[16,8,128]{2,1,0:T(8,128)S(1)} %get-tuple-element.96), channel_id=1, source_target_pairs={{0,16},{1,17},{2,18},{3,19},{4,20},{5,21},{6,22},{7,23},{8,24},{9,... | collective-permute-start | bytes 196616 | tf_op jit(solution)/shard_map/ppermute | solution.py:598
  29.2 1.8 %shard_map.80.send_ref = bf16[640,1024]{1,0:T(8,128)(2,1)S(1)} custom-call(s32[3]{0:T(128)S(1)} %pad_add_fusion.2.place_ref, s32[16,384]{1,0:T(8,128)S(1)} %get-tuple-element.102.holder_ref, s32[16,384]{1,0:T(8,128)S(1)} %get-tuple-element.121.spot_ref), custom_call_target="tpu_custom_call" | custom-call | tf_op jit(solution)/shard_map/pallas_call | solution.py:611
  31.0 3.3 %all-to-all-done.3.got_ref = f32[32,1,1152]{2,1,0:T(1,128)S(1)} async-done(((f32[32,1,1152]{2,1,0:T(1,128)}), f32[32,1,1152]{2,1,0:T(1,128)S(1)}, u32[]{:S(2)}, u32[]{:S(2)}) %all-to-all-start.3) | async-done | bytes 147488 | tf_op jit(solution)/shard_map/all_to_all | solution.py:661
  34.3 1.7 %shard_map.81 = (f32[16,16,128]{2,1,0:T(8,128)}, f32[2,32,128]{2,1,0:T(8,128)S(1)}) custom-call(s32[3]{0:T(128)S(1)} %pad_add_fusion.2.place_ref, f32[32,1,1152]{2,1,0:T(1,128)S(1)} %all-to-all-done.3.got_ref, bf16[640,1024]{1,0:T(8,128)(2,1)S(1)} %shard_map.80.send_ref, f32[16,24,128]{2,1,0:T(8,128)S(1)} %get-tuple-element.93.lower_ref, ...), custom_call_target="tpu_custom_call" | custom-call | tf_op jit(solution)/shard_map/pallas_call | solution.py:611
  36.0 10.7 %all-to-all-start.4 = ((f32[16,16,128]{2,1,0:T(8,128)}), f32[16,16,128]{2,1,0:T(8,128)S(1)}, u32[]{:S(2)}, u32[]{:S(2)}) async-start(f32[16,16,128]{2,1,0:T(8,128)} %get-tuple-element.101), calls=%async_computation.4 | async-start | bytes 262144 | tf_op jit(solution)/shard_map/all_to_all | solution.py:721
  46.7 3.4 %collective-permute-start.4 = (f32[2,32,128]{2,1,0:T(8,128)S(1)}, f32[2,32,128]{2,1,0:T(8,128)S(1)}, u32[]{:S(2)}, u32[]{:S(2)}) collective-permute-start(f32[2,32,128]{2,1,0:T(8,128)S(1)} %get-tuple-element.100), channel_id=1, source_target_pairs={{0,1},{1,2},{2,3},{3,4},{4,5},{5,6},{6,7},{7,8},{8,9},{9,10},{10,1... | collective-permute-start | bytes 98312 | tf_op jit(solution)/shard_map/ppermute | solution.py:598
  50.2 1.0 %shard_map.82 = (bf16[1024,384]{1,0:T(8,128)(2,1)S(1)}, f32[5,32,128]{2,1,0:T(8,128)S(1)}) custom-call(s32[3]{0:T(128)S(1)} %pad_add_fusion.2.place_ref, s32[16,384]{1,0:T(8,128)S(1)} %get-tuple-element.102.holder_ref), custom_call_target="tpu_custom_call" | custom-call | tf_op jit(solution)/shard_map/pallas_call | solution.py:611
  51.7 4.2 %all-to-all-done.4.got_ref = f32[16,16,128]{2,1,0:T(8,128)S(1)} async-done(((f32[16,16,128]{2,1,0:T(8,128)}), f32[16,16,128]{2,1,0:T(8,128)S(1)}, u32[]{:S(2)}, u32[]{:S(2)}) %all-to-all-start.4) | async-done | bytes 131104 | tf_op jit(solution)/shard_map/all_to_all | solution.py:721
  55.9 2.2 %shard_map.84 = (f32[16,24,128]{2,1,0:T(8,128)S(1)}, f32[32,1,1152]{2,1,0:T(1,128)S(1)}) custom-call(s32[3]{0:T(128)S(1)} %pad_add_fusion.2.place_ref, f32[2]{0:T(128)S(1)} %copy-done.1, f32[16,24,128]{2,1,0:T(8,128)S(1)} %get-tuple-element.93.lower_ref, f32[16,8,128]{2,1,0:T(8,128)S(1)} %collective-permute-done.3.north_ref, ...), custom_call_target="tpu_custom_call" | custom-call | tf_op jit(solution)/shard_map/pallas_call | solution.py:611
  58.1 14.8 %all_to_all.35.got_ref = f32[32,1,1152]{2,1,0:T(1,128)S(1)} all-to-all(f32[32,1,1152]{2,1,0:T(1,128)S(1)} %get-tuple-element.107), channel_id=1, replica_groups=mesh['panel'=2,'lat'=16,'lon'=16] {'panel','lon'}, dimensions={0} | all-to-all | bytes 294912 | tf_op jit(solution)/shard_map/all_to_all | solution.py:661
  72.9 1.7 %shard_map.85 = f32[16,16,128]{2,1,0:T(8,128)} custom-call(s32[3]{0:T(128)S(1)} %pad_add_fusion.2.place_ref, f32[32,1,1152]{2,1,0:T(1,128)S(1)} %all_to_all.35.got_ref, bf16[640,1024]{1,0:T(8,128)(2,1)S(1)} %shard_map.80.send_ref), custom_call_target="tpu_custom_call" | custom-call | tf_op jit(solution)/shard_map/pallas_call | solution.py:611
  74.6 6.5 %all-to-all-start.6 = ((f32[16,16,128]{2,1,0:T(8,128)}), f32[16,16,128]{2,1,0:T(8,128)S(1)}, u32[]{:S(2)}, u32[]{:S(2)}) async-start(f32[16,16,128]{2,1,0:T(8,128)} %shard_map.85), calls=%async_computation.6 | async-start | bytes 262144 | tf_op jit(solution)/shard_map/all_to_all | solution.py:721
  81.1 0.7 fusion.4
  83.1 7.2 %all-to-all-done.6.got_ref = f32[16,16,128]{2,1,0:T(8,128)S(1)} async-done(((f32[16,16,128]{2,1,0:T(8,128)}), f32[16,16,128]{2,1,0:T(8,128)S(1)}, u32[]{:S(2)}, u32[]{:S(2)}) %all-to-all-start.6) | async-done | bytes 131104 | tf_op jit(solution)/shard_map/all_to_all | solution.py:721
  90.3 2.7 %shard_map.86 = (f32[8,4,16,48]{3,2,1,0:T(8,128)}, f32[8,4,16,48]{3,2,1,0:T(8,128)}) custom-call(s32[3]{0:T(128)S(1)} %pad_add_fusion.2.place_ref, f32[2]{0:T(128)S(1)} %copy-done.1, f32[16,24,128]{2,1,0:T(8,128)S(1)} %get-tuple-element.108.middle_ref, f32[16,16,128]{2,1,0:T(8,128)S(1)} %all-to-all-done.6.got_ref, ...), custom_call_target="tpu_custom_call" | custom-call | tf_op jit(solution)/shard_map/pallas_call | solution.py:611
  (32 shorter events, 2.7 us)
Async XLA Ops:
  0.6 1.0 %copy-start = (f32[1,8,4,16,48]{4,3,2,1,0:T(8,128)S(1)}, f32[1,8,4,16,48]{4,3,2,1,0:T(8,128)}, u32[]{:S(2)}) copy-start(f32[1,8,4,16,48]{4,3,2,1,0:T(8,128)} %param.8) | copy-start | bytes 294916
  1.8 13.0 %collective-permute-start.2 = (f32[2,8,128]{2,1,0:T(8,128)S(1)}, f32[2,8,128]{2,1,0:T(8,128)S(1)}, u32[]{:S(2)}, u32[]{:S(2)}) collective-permute-start(f32[2,8,128]{2,1,0:T(8,128)S(1)} %get-tuple-element.89), channel_id=1, source_target_pairs={{17,0},{18,1},{19,2},{20,3},{21,4},{22,5},{23,6},{24,7},{25,8},{26... | collective-permute-start | bytes 24584 | tf_op jit(solution)/shard_map/ppermute | solution.py:598
  3.1 12.2 %collective-permute-start.1 = (f32[2,16,128]{2,1,0:T(8,128)S(1)}, f32[2,16,128]{2,1,0:T(8,128)S(1)}, u32[]{:S(2)}, u32[]{:S(2)}) collective-permute-start(f32[2,16,128]{2,1,0:T(8,128)S(1)} %get-tuple-element.88), channel_id=1, source_target_pairs={{1,0},{2,1},{3,2},{4,3},{5,4},{6,5},{7,6},{8,7},{9,8},{10,9},{11,1... | collective-permute-start | bytes 49160 | tf_op jit(solution)/shard_map/ppermute | solution.py:598
  4.4 10.9 %collective-permute-start = (f32[16,8,128]{2,1,0:T(8,128)S(1)}, f32[16,8,128]{2,1,0:T(8,128)S(1)}, u32[]{:S(2)}, u32[]{:S(2)}) collective-permute-start(f32[16,8,128]{2,1,0:T(8,128)S(1)} %get-tuple-element.87), channel_id=1, source_target_pairs={{16,0},{17,1},{18,2},{19,3},{20,4},{21,5},{22,6},{23,7},{24,8},{25... | collective-permute-start | bytes 196616 | tf_op jit(solution)/shard_map/ppermute | solution.py:598
  17.1 17.3 %all-to-all-start.3 = ((f32[32,1,1152]{2,1,0:T(1,128)}), f32[32,1,1152]{2,1,0:T(1,128)S(1)}, u32[]{:S(2)}, u32[]{:S(2)}) async-start(f32[32,1,1152]{2,1,0:T(1,128)} %get-tuple-element.95), calls=%async_computation.3 | async-start | bytes 294912 | tf_op jit(solution)/shard_map/all_to_all | solution.py:661
  26.2 4.8 %collective-permute-start.3 = (f32[16,8,128]{2,1,0:T(8,128)S(1)}, f32[16,8,128]{2,1,0:T(8,128)S(1)}, u32[]{:S(2)}, u32[]{:S(2)}) collective-permute-start(f32[16,8,128]{2,1,0:T(8,128)S(1)} %get-tuple-element.96), channel_id=1, source_target_pairs={{0,16},{1,17},{2,18},{3,19},{4,20},{5,21},{6,22},{7,23},{8,24},{9,... | collective-permute-start | bytes 196616 | tf_op jit(solution)/shard_map/ppermute | solution.py:598
  31.0 24.9 %copy-start.1 = (f32[2]{0:T(128)S(1)}, f32[2]{0:T(128)}, u32[]{:S(2)}) copy-start(f32[2]{0:T(128)} %diffusion_ref.3) | copy-start | bytes 28
  36.0 19.9 %all-to-all-start.4 = ((f32[16,16,128]{2,1,0:T(8,128)}), f32[16,16,128]{2,1,0:T(8,128)S(1)}, u32[]{:S(2)}, u32[]{:S(2)}) async-start(f32[16,16,128]{2,1,0:T(8,128)} %get-tuple-element.101), calls=%async_computation.4 | async-start | bytes 262144 | tf_op jit(solution)/shard_map/all_to_all | solution.py:721
  46.7 4.9 %collective-permute-start.4 = (f32[2,32,128]{2,1,0:T(8,128)S(1)}, f32[2,32,128]{2,1,0:T(8,128)S(1)}, u32[]{:S(2)}, u32[]{:S(2)}) collective-permute-start(f32[2,32,128]{2,1,0:T(8,128)S(1)} %get-tuple-element.100), channel_id=1, source_target_pairs={{0,1},{1,2},{2,3},{3,4},{4,5},{5,6},{6,7},{7,8},{8,9},{9,10},{10,1... | collective-permute-start | bytes 98312 | tf_op jit(solution)/shard_map/ppermute | solution.py:598
  74.6 15.6 %all-to-all-start.6 = ((f32[16,16,128]{2,1,0:T(8,128)}), f32[16,16,128]{2,1,0:T(8,128)S(1)}, u32[]{:S(2)}, u32[]{:S(2)}) async-start(f32[16,16,128]{2,1,0:T(8,128)} %shard_map.85), calls=%async_computation.6 | async-start | bytes 262144 | tf_op jit(solution)/shard_map/all_to_all | solution.py:721

commit v4 on v3

--- a/solution.py
+++ b/solution.py
@@ -663,9 +663,8 @@
     got = to_holders(sent)
 
     north, late_lat, late_lon, border, _ = lax.optimization_barrier(
-        (north, lat, lon, border_source, sent)
-    )
-    border = lax.optimization_barrier(border[0])
+        (north, lat, lon, border_source[0], sent)
+    )
     north = shift(north, 1, 0)
 
     ring = PANEL_COLS + 8

time: 93.6 us -> 93.3 us (level)
  starting transfers between devices: 41.9 us -> 43.2 us
  blocking collectives: 14.8 us -> 13.8 us
    all_to_all x1, blocking collectives: 14.8 us -> 13.8 us  [to_holders(): return lax.all_to_all(sent, ('panel', 'lon'), 0, 0, tiled=True)]
  transfers between devices with their start and end apart: 8 -> 8, of which waited for: 4 -> 3; matrix products, arithmetic and copies ran while one was open for 5% -> 4% of each run, Pallas kernels for 4% -> 4%
where the time goes in v4:
time: 93.3 us; the launch traced here: 92.7 us
  starting transfers between devices  43.2 us (46%)
  waiting for transfers between devices  14.8 us (16%)
  blocking collectives  13.8 us (15%)
  Pallas kernels  13.6 us (15%)
  local copies, waits for them, and re-layouts  2.62 us (3%)
  other arithmetic  2.55 us (3%)
  between operations  2.21 us (2%)
    all_to_all x2, starting transfers between devices, to_blocks(): return lax.all_to_all(chunks, 'lat', 0, 0, tiled=True)  17.9 us
    ppermute x5, starting transfers between devices, shift(): return lax.ppermute(value, ('lat', 'lon'), pairs)  17.7 us
    all_to_all x1, blocking collectives, to_holders(): return lax.all_to_all(sent, ('panel', 'lon'), 0, 0, tiled=True)  13.8 us
    pallas_call x10, Pallas kernels, call(): pl.pallas_call(kernel, out_shape=shapes, in_specs=specs or [SMEM] * smem...  13.6 us
    all_to_all x2, waiting for transfers between devices, to_blocks(): return lax.all_to_all(chunks, 'lat', 0, 0, tiled=True)  11.2 us
    all_to_all x1, starting transfers between devices, to_holders(): return lax.all_to_all(sent, ('panel', 'lon'), 0, 0, tiled=True)  7.51 us
    all_to_all x1, waiting for transfers between devices, to_holders(): return lax.all_to_all(sent, ('panel', 'lon'), 0, 0, tiled=True)  3.59 us
  transfers between devices with their start and end apart: 8, of which 3 were waited for; matrix products, arithmetic and copies ran while one was open for 4% of the time, Pallas kernels for 4%

profile of v4, /device:TPU:1, one launch (start us, length us, event | category | flops | bytes accessed | tf_op | source)
XLA Modules:
  0.0 92.7 jit_solution(18405769318053001665)
XLA Ops:
  0.6 0.9 %copy-done = f32[1,8,4,16,48]{4,3,2,1,0:T(8,128)S(1)} copy-done((f32[1,8,4,16,48]{4,3,2,1,0:T(8,128)S(1)}, f32[1,8,4,16,48]{4,3,2,1,0:T(8,128)}, u32[]{:S(2)}) %copy-start) | copy-done | bytes 98328
  1.8 1.3 %collective-permute-start.2 = (f32[2,8,128]{2,1,0:T(8,128)S(1)}, f32[2,8,128]{2,1,0:T(8,128)S(1)}, u32[]{:S(2)}, u32[]{:S(2)}) collective-permute-start(f32[2,8,128]{2,1,0:T(8,128)S(1)} %get-tuple-element.89), channel_id=1, source_target_pairs={{17,0},{18,1},{19,2},{20,3},{21,4},{22,5},{23,6},{24,7},{25,8},{26... | collective-permute-start | bytes 24584 | tf_op jit(solution)/shard_map/ppermute | solution.py:598
  3.1 1.3 %collective-permute-start.1 = (f32[2,16,128]{2,1,0:T(8,128)S(1)}, f32[2,16,128]{2,1,0:T(8,128)S(1)}, u32[]{:S(2)}, u32[]{:S(2)}) collective-permute-start(f32[2,16,128]{2,1,0:T(8,128)S(1)} %get-tuple-element.88), channel_id=1, source_target_pairs={{1,0},{2,1},{3,2},{4,3},{5,4},{6,5},{7,6},{8,7},{9,8},{10,9},{11,1... | collective-permute-start | bytes 49160 | tf_op jit(solution)/shard_map/ppermute | solution.py:598
  4.4 8.8 %collective-permute-start = (f32[16,8,128]{2,1,0:T(8,128)S(1)}, f32[16,8,128]{2,1,0:T(8,128)S(1)}, u32[]{:S(2)}, u32[]{:S(2)}) collective-permute-start(f32[16,8,128]{2,1,0:T(8,128)S(1)} %get-tuple-element.87), channel_id=1, source_target_pairs={{16,0},{17,1},{18,2},{19,3},{20,4},{21,5},{22,6},{23,7},{24,8},{25... | collective-permute-start | bytes 196616 | tf_op jit(solution)/shard_map/ppermute | solution.py:598
  13.2 0.7 convert_bitcast_fusion
  13.9 0.7 pad_maximum_fusion.donor_ref
  14.8 0.8 reduce
  15.7 1.8 %shard_map.79 = (f32[16,24,128]{2,1,0:T(8,128)S(1)}, f32[16,8,128]{2,1,0:T(8,128)S(1)}, f32[32,1,1152]{2,1,0:T(1,128)}) custom-call(s32[3]{0:T(128)S(1)} %pad_add_fusion.2.place_ref, f32[16,16,128]{2,1,0:T(8,128)S(1)} %get-tuple-element.86.held_ref, f32[16,8,128]{2,1,0:T(8,128)S(1)} %collective-permute-done.south_ref, ...), custom_call_target="tpu_custom_call" | custom-call | tf_op jit(solution)/shard_map/pallas_call | solution.py:611
  17.5 7.5 %all-to-all-start.3 = ((f32[32,1,1152]{2,1,0:T(1,128)}), f32[32,1,1152]{2,1,0:T(1,128)S(1)}, u32[]{:S(2)}, u32[]{:S(2)}) async-start(f32[32,1,1152]{2,1,0:T(1,128)} %get-tuple-element.95), calls=%async_computation.3 | async-start | bytes 294912 | tf_op jit(solution)/shard_map/all_to_all | solution.py:661
  25.4 2.8 %collective-permute-start.3 = (f32[16,8,128]{2,1,0:T(8,128)S(1)}, f32[16,8,128]{2,1,0:T(8,128)S(1)}, u32[]{:S(2)}, u32[]{:S(2)}) collective-permute-start(f32[16,8,128]{2,1,0:T(8,128)S(1)} %get-tuple-element.96), channel_id=1, source_target_pairs={{0,16},{1,17},{2,18},{3,19},{4,20},{5,21},{6,22},{7,23},{8,24},{9,... | collective-permute-start | bytes 196616 | tf_op jit(solution)/shard_map/ppermute | solution.py:598
  29.0 1.8 %shard_map.80.send_ref = bf16[640,1024]{1,0:T(8,128)(2,1)S(1)} custom-call(s32[3]{0:T(128)S(1)} %pad_add_fusion.2.place_ref, s32[16,384]{1,0:T(8,128)S(1)} %get-tuple-element.102.holder_ref, s32[16,384]{1,0:T(8,128)S(1)} %get-tuple-element.121.spot_ref), custom_call_target="tpu_custom_call" | custom-call | tf_op jit(solution)/shard_map/pallas_call | solution.py:611
  30.8 3.6 %all-to-all-done.3.got_ref = f32[32,1,1152]{2,1,0:T(1,128)S(1)} async-done(((f32[32,1,1152]{2,1,0:T(1,128)}), f32[32,1,1152]{2,1,0:T(1,128)S(1)}, u32[]{:S(2)}, u32[]{:S(2)}) %all-to-all-start.3) | async-done | bytes 147488 | tf_op jit(solution)/shard_map/all_to_all | solution.py:661
  34.4 1.7 %shard_map.81 = (f32[16,16,128]{2,1,0:T(8,128)}, f32[2,32,128]{2,1,0:T(8,128)S(1)}) custom-call(s32[3]{0:T(128)S(1)} %pad_add_fusion.2.place_ref, f32[32,1,1152]{2,1,0:T(1,128)S(1)} %all-to-all-done.3.got_ref, bf16[640,1024]{1,0:T(8,128)(2,1)S(1)} %shard_map.80.send_ref, f32[16,24,128]{2,1,0:T(8,128)S(1)} %get-tuple-element.93.lower_ref, ...), custom_call_target="tpu_custom_call" | custom-call | tf_op jit(solution)/shard_map/pallas_call | solution.py:611
  36.1 11.5 %all-to-all-start.4 = ((f32[16,16,128]{2,1,0:T(8,128)}), f32[16,16,128]{2,1,0:T(8,128)S(1)}, u32[]{:S(2)}, u32[]{:S(2)}) async-start(f32[16,16,128]{2,1,0:T(8,128)} %get-tuple-element.101), calls=%async_computation.4 | async-start | bytes 262144 | tf_op jit(solution)/shard_map/all_to_all | solution.py:720
  47.5 3.6 %collective-permute-start.4 = (f32[2,32,128]{2,1,0:T(8,128)S(1)}, f32[2,32,128]{2,1,0:T(8,128)S(1)}, u32[]{:S(2)}, u32[]{:S(2)}) collective-permute-start(f32[2,32,128]{2,1,0:T(8,128)S(1)} %get-tuple-element.100), channel_id=1, source_target_pairs={{0,1},{1,2},{2,3},{3,4},{4,5},{5,6},{6,7},{7,8},{8,9},{9,10},{10,1... | collective-permute-start | bytes 98312 | tf_op jit(solution)/shard_map/ppermute | solution.py:598
  51.2 1.0 %shard_map.82 = (bf16[1024,384]{1,0:T(8,128)(2,1)S(1)}, f32[5,32,128]{2,1,0:T(8,128)S(1)}) custom-call(s32[3]{0:T(128)S(1)} %pad_add_fusion.2.place_ref, s32[16,384]{1,0:T(8,128)S(1)} %get-tuple-element.102.holder_ref), custom_call_target="tpu_custom_call" | custom-call | tf_op jit(solution)/shard_map/pallas_call | solution.py:611
  52.7 4.0 %all-to-all-done.4.got_ref = f32[16,16,128]{2,1,0:T(8,128)S(1)} async-done(((f32[16,16,128]{2,1,0:T(8,128)}), f32[16,16,128]{2,1,0:T(8,128)S(1)}, u32[]{:S(2)}, u32[]{:S(2)}) %all-to-all-start.4) | async-done | bytes 131104 | tf_op jit(solution)/shard_map/all_to_all | solution.py:720
  56.7 2.2 %shard_map.84 = (f32[16,24,128]{2,1,0:T(8,128)S(1)}, f32[32,1,1152]{2,1,0:T(1,128)S(1)}) custom-call(s32[3]{0:T(128)S(1)} %pad_add_fusion.2.place_ref, f32[2]{0:T(128)S(1)} %copy-done.1, f32[16,24,128]{2,1,0:T(8,128)S(1)} %get-tuple-element.93.lower_ref, f32[16,8,128]{2,1,0:T(8,128)S(1)} %collective-permute-done.3.north_ref, ...), custom_call_target="tpu_custom_call" | custom-call | tf_op jit(solution)/shard_map/pallas_call | solution.py:611
  58.9 13.8 %all_to_all.35.got_ref = f32[32,1,1152]{2,1,0:T(1,128)S(1)} all-to-all(f32[32,1,1152]{2,1,0:T(1,128)S(1)} %get-tuple-element.107), channel_id=1, replica_groups=mesh['panel'=2,'lat'=16,'lon'=16] {'panel','lon'}, dimensions={0} | all-to-all | bytes 294912 | tf_op jit(solution)/shard_map/all_to_all | solution.py:661
  72.7 1.7 %shard_map.85 = f32[16,16,128]{2,1,0:T(8,128)} custom-call(s32[3]{0:T(128)S(1)} %pad_add_fusion.2.place_ref, f32[32,1,1152]{2,1,0:T(1,128)S(1)} %all_to_all.35.got_ref, bf16[640,1024]{1,0:T(8,128)(2,1)S(1)} %shard_map.80.send_ref), custom_call_target="tpu_custom_call" | custom-call | tf_op jit(solution)/shard_map/pallas_call | solution.py:611
  74.4 6.5 %all-to-all-start.6 = ((f32[16,16,128]{2,1,0:T(8,128)}), f32[16,16,128]{2,1,0:T(8,128)S(1)}, u32[]{:S(2)}, u32[]{:S(2)}) async-start(f32[16,16,128]{2,1,0:T(8,128)} %shard_map.85), calls=%async_computation.6 | async-start | bytes 262144 | tf_op jit(solution)/shard_map/all_to_all | solution.py:720
  80.9 0.7 fusion.4
  82.9 7.2 %all-to-all-done.6.got_ref = f32[16,16,128]{2,1,0:T(8,128)S(1)} async-done(((f32[16,16,128]{2,1,0:T(8,128)}), f32[16,16,128]{2,1,0:T(8,128)S(1)}, u32[]{:S(2)}, u32[]{:S(2)}) %all-to-all-start.6) | async-done | bytes 131104 | tf_op jit(solution)/shard_map/all_to_all | solution.py:720
  90.0 2.7 %shard_map.86 = (f32[8,4,16,48]{3,2,1,0:T(8,128)}, f32[8,4,16,48]{3,2,1,0:T(8,128)}) custom-call(s32[3]{0:T(128)S(1)} %pad_add_fusion.2.place_ref, f32[2]{0:T(128)S(1)} %copy-done.1, f32[16,24,128]{2,1,0:T(8,128)S(1)} %get-tuple-element.108.middle_ref, f32[16,16,128]{2,1,0:T(8,128)S(1)} %all-to-all-done.6.got_ref, ...), custom_call_target="tpu_custom_call" | custom-call | tf_op jit(solution)/shard_map/pallas_call | solution.py:611
  (32 shorter events, 2.2 us)
Async XLA Ops:
  0.6 1.0 %copy-start = (f32[1,8,4,16,48]{4,3,2,1,0:T(8,128)S(1)}, f32[1,8,4,16,48]{4,3,2,1,0:T(8,128)}, u32[]{:S(2)}) copy-start(f32[1,8,4,16,48]{4,3,2,1,0:T(8,128)} %param.8) | copy-start | bytes 294916
  1.8 13.9 %collective-permute-start.2 = (f32[2,8,128]{2,1,0:T(8,128)S(1)}, f32[2,8,128]{2,1,0:T(8,128)S(1)}, u32[]{:S(2)}, u32[]{:S(2)}) collective-permute-start(f32[2,8,128]{2,1,0:T(8,128)S(1)} %get-tuple-element.89), channel_id=1, source_target_pairs={{17,0},{18,1},{19,2},{20,3},{21,4},{22,5},{23,6},{24,7},{25,8},{26... | collective-permute-start | bytes 24584 | tf_op jit(solution)/shard_map/ppermute | solution.py:598
  3.1 12.6 %collective-permute-start.1 = (f32[2,16,128]{2,1,0:T(8,128)S(1)}, f32[2,16,128]{2,1,0:T(8,128)S(1)}, u32[]{:S(2)}, u32[]{:S(2)}) collective-permute-start(f32[2,16,128]{2,1,0:T(8,128)S(1)} %get-tuple-element.88), channel_id=1, source_target_pairs={{1,0},{2,1},{3,2},{4,3},{5,4},{6,5},{7,6},{8,7},{9,8},{10,9},{11,1... | collective-permute-start | bytes 49160 | tf_op jit(solution)/shard_map/ppermute | solution.py:598
  4.4 11.3 %collective-permute-start = (f32[16,8,128]{2,1,0:T(8,128)S(1)}, f32[16,8,128]{2,1,0:T(8,128)S(1)}, u32[]{:S(2)}, u32[]{:S(2)}) collective-permute-start(f32[16,8,128]{2,1,0:T(8,128)S(1)} %get-tuple-element.87), channel_id=1, source_target_pairs={{16,0},{17,1},{18,2},{19,3},{20,4},{21,5},{22,6},{23,7},{24,8},{25... | collective-permute-start | bytes 196616 | tf_op jit(solution)/shard_map/ppermute | solution.py:598
  17.5 16.9 %all-to-all-start.3 = ((f32[32,1,1152]{2,1,0:T(1,128)}), f32[32,1,1152]{2,1,0:T(1,128)S(1)}, u32[]{:S(2)}, u32[]{:S(2)}) async-start(f32[32,1,1152]{2,1,0:T(1,128)} %get-tuple-element.95), calls=%async_computation.3 | async-start | bytes 294912 | tf_op jit(solution)/shard_map/all_to_all | solution.py:661
  25.4 5.4 %collective-permute-start.3 = (f32[16,8,128]{2,1,0:T(8,128)S(1)}, f32[16,8,128]{2,1,0:T(8,128)S(1)}, u32[]{:S(2)}, u32[]{:S(2)}) collective-permute-start(f32[16,8,128]{2,1,0:T(8,128)S(1)} %get-tuple-element.96), channel_id=1, source_target_pairs={{0,16},{1,17},{2,18},{3,19},{4,20},{5,21},{6,22},{7,23},{8,24},{9,... | collective-permute-start | bytes 196616 | tf_op jit(solution)/shard_map/ppermute | solution.py:598
  30.7 25.9 %copy-start.1 = (f32[2]{0:T(128)S(1)}, f32[2]{0:T(128)}, u32[]{:S(2)}) copy-start(f32[2]{0:T(128)} %diffusion_ref.3) | copy-start | bytes 28
  36.1 20.6 %all-to-all-start.4 = ((f32[16,16,128]{2,1,0:T(8,128)}), f32[16,16,128]{2,1,0:T(8,128)S(1)}, u32[]{:S(2)}, u32[]{:S(2)}) async-start(f32[16,16,128]{2,1,0:T(8,128)} %get-tuple-element.101), calls=%async_computation.4 | async-start | bytes 262144 | tf_op jit(solution)/shard_map/all_to_all | solution.py:720
  47.5 5.2 %collective-permute-start.4 = (f32[2,32,128]{2,1,0:T(8,128)S(1)}, f32[2,32,128]{2,1,0:T(8,128)S(1)}, u32[]{:S(2)}, u32[]{:S(2)}) collective-permute-start(f32[2,32,128]{2,1,0:T(8,128)S(1)} %get-tuple-element.100), channel_id=1, source_target_pairs={{0,1},{1,2},{2,3},{3,4},{4,5},{5,6},{6,7},{7,8},{8,9},{9,10},{10,1... | collective-permute-start | bytes 98312 | tf_op jit(solution)/shard_map/ppermute | solution.py:598
  74.4 15.6 %all-to-all-start.6 = ((f32[16,16,128]{2,1,0:T(8,128)}), f32[16,16,128]{2,1,0:T(8,128)S(1)}, u32[]{:S(2)}, u32[]{:S(2)}) async-start(f32[16,16,128]{2,1,0:T(8,128)} %shard_map.85), calls=%async_computation.6 | async-start | bytes 262144 | tf_op jit(solution)/shard_map/all_to_all | solution.py:720

commit v5 on v3

--- a/solution.py
+++ b/solution.py
@@ -629,8 +629,8 @@
         fields,
         scratch=[pltpu.VMEM((PLANES, ROWS, WIDE), f32)],
     )
+    east = shift(east, 0, -1)
     south = shift(south, -1, 0)
-    east = shift(east, 0, -1)
     corner = shift(corner, -1, -1)
 
     donor = jnp.concatenate(

time: 93.6 us -> 93.6 us (level)
  no operation moved by 1% of the time
where the time goes in v5:
time: 93.6 us; the launch traced here: 92.9 us
  starting transfers between devices  41.9 us (45%)
  waiting for transfers between devices  15.2 us (16%)
  blocking collectives  14.8 us (16%)
  Pallas kernels  13.6 us (15%)
  local copies, waits for them, and re-layouts  2.62 us (3%)
  other arithmetic  2.55 us (3%)
  between operations  2.19 us (2%)
    all_to_all x2, starting transfers between devices, to_blocks(): return lax.all_to_all(chunks, 'lat', 0, 0, tiled=True)  17.2 us
    ppermute x5, starting transfers between devices, shift(): return lax.ppermute(value, ('lat', 'lon'), pairs)  16.9 us
    all_to_all x1, blocking collectives, to_holders(): return lax.all_to_all(sent, ('panel', 'lon'), 0, 0, tiled=True)  14.8 us
    pallas_call x10, Pallas kernels, call(): pl.pallas_call(kernel, out_shape=shapes, in_specs=specs or [SMEM] * smem...  13.6 us
    all_to_all x2, waiting for transfers between devices, to_blocks(): return lax.all_to_all(chunks, 'lat', 0, 0, tiled=True)  11.4 us
    all_to_all x1, starting transfers between devices, to_holders(): return lax.all_to_all(sent, ('panel', 'lon'), 0, 0, tiled=True)  7.87 us
    all_to_all x1, waiting for transfers between devices, to_holders(): return lax.all_to_all(sent, ('panel', 'lon'), 0, 0, tiled=True)  3.34 us
  transfers between devices with their start and end apart: 8, of which 4 were waited for; matrix products, arithmetic and copies ran while one was open for 5% of the time, Pallas kernels for 4%

profile of v5, /device:TPU:1, one launch (start us, length us, event | category | flops | bytes accessed | tf_op | source)
XLA Modules:
  0.0 92.9 jit_solution(7618489564706478320)
XLA Ops:
  0.6 0.9 %copy-done = f32[1,8,4,16,48]{4,3,2,1,0:T(8,128)S(1)} copy-done((f32[1,8,4,16,48]{4,3,2,1,0:T(8,128)S(1)}, f32[1,8,4,16,48]{4,3,2,1,0:T(8,128)}, u32[]{:S(2)}) %copy-start) | copy-done | bytes 98328
  1.8 1.3 %collective-permute-start.2 = (f32[2,8,128]{2,1,0:T(8,128)S(1)}, f32[2,8,128]{2,1,0:T(8,128)S(1)}, u32[]{:S(2)}, u32[]{:S(2)}) collective-permute-start(f32[2,8,128]{2,1,0:T(8,128)S(1)} %get-tuple-element.89), channel_id=1, source_target_pairs={{17,0},{18,1},{19,2},{20,3},{21,4},{22,5},{23,6},{24,7},{25,8},{26... | collective-permute-start | bytes 24584 | tf_op jit(solution)/shard_map/ppermute | solution.py:598
  3.1 1.3 %collective-permute-start.1 = (f32[2,16,128]{2,1,0:T(8,128)S(1)}, f32[2,16,128]{2,1,0:T(8,128)S(1)}, u32[]{:S(2)}, u32[]{:S(2)}) collective-permute-start(f32[2,16,128]{2,1,0:T(8,128)S(1)} %get-tuple-element.88), channel_id=1, source_target_pairs={{1,0},{2,1},{3,2},{4,3},{5,4},{6,5},{7,6},{8,7},{9,8},{10,9},{11,1... | collective-permute-start | bytes 49160 | tf_op jit(solution)/shard_map/ppermute | solution.py:598
  4.4 8.8 %collective-permute-start = (f32[16,8,128]{2,1,0:T(8,128)S(1)}, f32[16,8,128]{2,1,0:T(8,128)S(1)}, u32[]{:S(2)}, u32[]{:S(2)}) collective-permute-start(f32[16,8,128]{2,1,0:T(8,128)S(1)} %get-tuple-element.87), channel_id=1, source_target_pairs={{16,0},{17,1},{18,2},{19,3},{20,4},{21,5},{22,6},{23,7},{24,8},{25... | collective-permute-start | bytes 196616 | tf_op jit(solution)/shard_map/ppermute | solution.py:598
  13.2 0.7 convert_bitcast_fusion
  13.9 0.7 pad_maximum_fusion.donor_ref
  15.3 1.8 %shard_map.79 = (f32[16,24,128]{2,1,0:T(8,128)S(1)}, f32[16,8,128]{2,1,0:T(8,128)S(1)}, f32[32,1,1152]{2,1,0:T(1,128)}) custom-call(s32[3]{0:T(128)S(1)} %pad_add_fusion.2.place_ref, f32[16,16,128]{2,1,0:T(8,128)S(1)} %get-tuple-element.86.held_ref, f32[16,8,128]{2,1,0:T(8,128)S(1)} %collective-permute-done.south_ref, ...), custom_call_target="tpu_custom_call" | custom-call | tf_op jit(solution)/shard_map/pallas_call | solution.py:611
  17.1 7.9 %all-to-all-start.3 = ((f32[32,1,1152]{2,1,0:T(1,128)}), f32[32,1,1152]{2,1,0:T(1,128)S(1)}, u32[]{:S(2)}, u32[]{:S(2)}) async-start(f32[32,1,1152]{2,1,0:T(1,128)} %get-tuple-element.95), calls=%async_computation.3 | async-start | bytes 294912 | tf_op jit(solution)/shard_map/all_to_all | solution.py:661
  24.9 0.8 reduce
  26.2 2.1 %collective-permute-start.3 = (f32[16,8,128]{2,1,0:T(8,128)S(1)}, f32[16,8,128]{2,1,0:T(8,128)S(1)}, u32[]{:S(2)}, u32[]{:S(2)}) collective-permute-start(f32[16,8,128]{2,1,0:T(8,128)S(1)} %get-tuple-element.96), channel_id=1, source_target_pairs={{0,16},{1,17},{2,18},{3,19},{4,20},{5,21},{6,22},{7,23},{8,24},{9,... | collective-permute-start | bytes 196616 | tf_op jit(solution)/shard_map/ppermute | solution.py:598
  29.2 1.8 %shard_map.80.send_ref = bf16[640,1024]{1,0:T(8,128)(2,1)S(1)} custom-call(s32[3]{0:T(128)S(1)} %pad_add_fusion.2.place_ref, s32[16,384]{1,0:T(8,128)S(1)} %get-tuple-element.102.holder_ref, s32[16,384]{1,0:T(8,128)S(1)} %get-tuple-element.121.spot_ref), custom_call_target="tpu_custom_call" | custom-call | tf_op jit(solution)/shard_map/pallas_call | solution.py:611
  31.0 3.3 %all-to-all-done.3.got_ref = f32[32,1,1152]{2,1,0:T(1,128)S(1)} async-done(((f32[32,1,1152]{2,1,0:T(1,128)}), f32[32,1,1152]{2,1,0:T(1,128)S(1)}, u32[]{:S(2)}, u32[]{:S(2)}) %all-to-all-start.3) | async-done | bytes 147488 | tf_op jit(solution)/shard_map/all_to_all | solution.py:661
  34.3 1.7 %shard_map.81 = (f32[16,16,128]{2,1,0:T(8,128)}, f32[2,32,128]{2,1,0:T(8,128)S(1)}) custom-call(s32[3]{0:T(128)S(1)} %pad_add_fusion.2.place_ref, f32[32,1,1152]{2,1,0:T(1,128)S(1)} %all-to-all-done.3.got_ref, bf16[640,1024]{1,0:T(8,128)(2,1)S(1)} %shard_map.80.send_ref, f32[16,24,128]{2,1,0:T(8,128)S(1)} %get-tuple-element.93.lower_ref, ...), custom_call_target="tpu_custom_call" | custom-call | tf_op jit(solution)/shard_map/pallas_call | solution.py:611
  36.0 10.7 %all-to-all-start.4 = ((f32[16,16,128]{2,1,0:T(8,128)}), f32[16,16,128]{2,1,0:T(8,128)S(1)}, u32[]{:S(2)}, u32[]{:S(2)}) async-start(f32[16,16,128]{2,1,0:T(8,128)} %get-tuple-element.101), calls=%async_computation.4 | async-start | bytes 262144 | tf_op jit(solution)/shard_map/all_to_all | solution.py:721
  46.7 3.4 %collective-permute-start.4 = (f32[2,32,128]{2,1,0:T(8,128)S(1)}, f32[2,32,128]{2,1,0:T(8,128)S(1)}, u32[]{:S(2)}, u32[]{:S(2)}) collective-permute-start(f32[2,32,128]{2,1,0:T(8,128)S(1)} %get-tuple-element.100), channel_id=1, source_target_pairs={{0,1},{1,2},{2,3},{3,4},{4,5},{5,6},{6,7},{7,8},{8,9},{9,10},{10,1... | collective-permute-start | bytes 98312 | tf_op jit(solution)/shard_map/ppermute | solution.py:598
  50.2 1.0 %shard_map.82 = (bf16[1024,384]{1,0:T(8,128)(2,1)S(1)}, f32[5,32,128]{2,1,0:T(8,128)S(1)}) custom-call(s32[3]{0:T(128)S(1)} %pad_add_fusion.2.place_ref, s32[16,384]{1,0:T(8,128)S(1)} %get-tuple-element.102.holder_ref), custom_call_target="tpu_custom_call" | custom-call | tf_op jit(solution)/shard_map/pallas_call | solution.py:611
  51.7 4.2 %all-to-all-done.4.got_ref = f32[16,16,128]{2,1,0:T(8,128)S(1)} async-done(((f32[16,16,128]{2,1,0:T(8,128)}), f32[16,16,128]{2,1,0:T(8,128)S(1)}, u32[]{:S(2)}, u32[]{:S(2)}) %all-to-all-start.4) | async-done | bytes 131104 | tf_op jit(solution)/shard_map/all_to_all | solution.py:721
  55.9 2.2 %shard_map.84 = (f32[16,24,128]{2,1,0:T(8,128)S(1)}, f32[32,1,1152]{2,1,0:T(1,128)S(1)}) custom-call(s32[3]{0:T(128)S(1)} %pad_add_fusion.2.place_ref, f32[2]{0:T(128)S(1)} %copy-done.1, f32[16,24,128]{2,1,0:T(8,128)S(1)} %get-tuple-element.93.lower_ref, f32[16,8,128]{2,1,0:T(8,128)S(1)} %collective-permute-done.3.north_ref, ...), custom_call_target="tpu_custom_call" | custom-call | tf_op jit(solution)/shard_map/pallas_call | solution.py:611
  58.1 14.8 %all_to_all.35.got_ref = f32[32,1,1152]{2,1,0:T(1,128)S(1)} all-to-all(f32[32,1,1152]{2,1,0:T(1,128)S(1)} %get-tuple-element.107), channel_id=1, replica_groups=mesh['panel'=2,'lat'=16,'lon'=16] {'panel','lon'}, dimensions={0} | all-to-all | bytes 294912 | tf_op jit(solution)/shard_map/all_to_all | solution.py:661
  72.9 1.7 %shard_map.85 = f32[16,16,128]{2,1,0:T(8,128)} custom-call(s32[3]{0:T(128)S(1)} %pad_add_fusion.2.place_ref, f32[32,1,1152]{2,1,0:T(1,128)S(1)} %all_to_all.35.got_ref, bf16[640,1024]{1,0:T(8,128)(2,1)S(1)} %shard_map.80.send_ref), custom_call_target="tpu_custom_call" | custom-call | tf_op jit(solution)/shard_map/pallas_call | solution.py:611
  74.6 6.5 %all-to-all-start.6 = ((f32[16,16,128]{2,1,0:T(8,128)}), f32[16,16,128]{2,1,0:T(8,128)S(1)}, u32[]{:S(2)}, u32[]{:S(2)}) async-start(f32[16,16,128]{2,1,0:T(8,128)} %shard_map.85), calls=%async_computation.6 | async-start | bytes 262144 | tf_op jit(solution)/shard_map/all_to_all | solution.py:721
  81.1 0.7 fusion.4
  83.1 7.2 %all-to-all-done.6.got_ref = f32[16,16,128]{2,1,0:T(8,128)S(1)} async-done(((f32[16,16,128]{2,1,0:T(8,128)}), f32[16,16,128]{2,1,0:T(8,128)S(1)}, u32[]{:S(2)}, u32[]{:S(2)}) %all-to-all-start.6) | async-done | bytes 131104 | tf_op jit(solution)/shard_map/all_to_all | solution.py:721
  90.3 2.7 %shard_map.86 = (f32[8,4,16,48]{3,2,1,0:T(8,128)}, f32[8,4,16,48]{3,2,1,0:T(8,128)}) custom-call(s32[3]{0:T(128)S(1)} %pad_add_fusion.2.place_ref, f32[2]{0:T(128)S(1)} %copy-done.1, f32[16,24,128]{2,1,0:T(8,128)S(1)} %get-tuple-element.108.middle_ref, f32[16,16,128]{2,1,0:T(8,128)S(1)} %all-to-all-done.6.got_ref, ...), custom_call_target="tpu_custom_call" | custom-call | tf_op jit(solution)/shard_map/pallas_call | solution.py:611
  (32 shorter events, 2.7 us)
Async XLA Ops:
  0.6 1.0 %copy-start = (f32[1,8,4,16,48]{4,3,2,1,0:T(8,128)S(1)}, f32[1,8,4,16,48]{4,3,2,1,0:T(8,128)}, u32[]{:S(2)}) copy-start(f32[1,8,4,16,48]{4,3,2,1,0:T(8,128)} %param.8) | copy-start | bytes 294916
  1.8 13.0 %collective-permute-start.2 = (f32[2,8,128]{2,1,0:T(8,128)S(1)}, f32[2,8,128]{2,1,0:T(8,128)S(1)}, u32[]{:S(2)}, u32[]{:S(2)}) collective-permute-start(f32[2,8,128]{2,1,0:T(8,128)S(1)} %get-tuple-element.89), channel_id=1, source_target_pairs={{17,0},{18,1},{19,2},{20,3},{21,4},{22,5},{23,6},{24,7},{25,8},{26... | collective-permute-start | bytes 24584 | tf_op jit(solution)/shard_map/ppermute | solution.py:598
  3.1 12.2 %collective-permute-start.1 = (f32[2,16,128]{2,1,0:T(8,128)S(1)}, f32[2,16,128]{2,1,0:T(8,128)S(1)}, u32[]{:S(2)}, u32[]{:S(2)}) collective-permute-start(f32[2,16,128]{2,1,0:T(8,128)S(1)} %get-tuple-element.88), channel_id=1, source_target_pairs={{1,0},{2,1},{3,2},{4,3},{5,4},{6,5},{7,6},{8,7},{9,8},{10,9},{11,1... | collective-permute-start | bytes 49160 | tf_op jit(solution)/shard_map/ppermute | solution.py:598
  4.4 10.9 %collective-permute-start = (f32[16,8,128]{2,1,0:T(8,128)S(1)}, f32[16,8,128]{2,1,0:T(8,128)S(1)}, u32[]{:S(2)}, u32[]{:S(2)}) collective-permute-start(f32[16,8,128]{2,1,0:T(8,128)S(1)} %get-tuple-element.87), channel_id=1, source_target_pairs={{16,0},{17,1},{18,2},{19,3},{20,4},{21,5},{22,6},{23,7},{24,8},{25... | collective-permute-start | bytes 196616 | tf_op jit(solution)/shard_map/ppermute | solution.py:598
  17.1 17.3 %all-to-all-start.3 = ((f32[32,1,1152]{2,1,0:T(1,128)}), f32[32,1,1152]{2,1,0:T(1,128)S(1)}, u32[]{:S(2)}, u32[]{:S(2)}) async-start(f32[32,1,1152]{2,1,0:T(1,128)} %get-tuple-element.95), calls=%async_computation.3 | async-start | bytes 294912 | tf_op jit(solution)/shard_map/all_to_all | solution.py:661
  26.2 4.8 %collective-permute-start.3 = (f32[16,8,128]{2,1,0:T(8,128)S(1)}, f32[16,8,128]{2,1,0:T(8,128)S(1)}, u32[]{:S(2)}, u32[]{:S(2)}) collective-permute-start(f32[16,8,128]{2,1,0:T(8,128)S(1)} %get-tuple-element.96), channel_id=1, source_target_pairs={{0,16},{1,17},{2,18},{3,19},{4,20},{5,21},{6,22},{7,23},{8,24},{9,... | collective-permute-start | bytes 196616 | tf_op jit(solution)/shard_map/ppermute | solution.py:598
  31.0 24.9 %copy-start.1 = (f32[2]{0:T(128)S(1)}, f32[2]{0:T(128)}, u32[]{:S(2)}) copy-start(f32[2]{0:T(128)} %diffusion_ref.3) | copy-start | bytes 28
  36.0 19.9 %all-to-all-start.4 = ((f32[16,16,128]{2,1,0:T(8,128)}), f32[16,16,128]{2,1,0:T(8,128)S(1)}, u32[]{:S(2)}, u32[]{:S(2)}) async-start(f32[16,16,128]{2,1,0:T(8,128)} %get-tuple-element.101), calls=%async_computation.4 | async-start | bytes 262144 | tf_op jit(solution)/shard_map/all_to_all | solution.py:721
  46.7 4.9 %collective-permute-start.4 = (f32[2,32,128]{2,1,0:T(8,128)S(1)}, f32[2,32,128]{2,1,0:T(8,128)S(1)}, u32[]{:S(2)}, u32[]{:S(2)}) collective-permute-start(f32[2,32,128]{2,1,0:T(8,128)S(1)} %get-tuple-element.100), channel_id=1, source_target_pairs={{0,1},{1,2},{2,3},{3,4},{4,5},{5,6},{6,7},{7,8},{8,9},{9,10},{10,1... | collective-permute-start | bytes 98312 | tf_op jit(solution)/shard_map/ppermute | solution.py:598
  74.6 15.6 %all-to-all-start.6 = ((f32[16,16,128]{2,1,0:T(8,128)}), f32[16,16,128]{2,1,0:T(8,128)S(1)}, u32[]{:S(2)}, u32[]{:S(2)}) async-start(f32[16,16,128]{2,1,0:T(8,128)} %shard_map.85), calls=%async_computation.6 | async-start | bytes 262144 | tf_op jit(solution)/shard_map/all_to_all | solution.py:721
